TPU v7x, 128 devices: a whole 4x4x4 slice. The times are simulated.
128 devices in a mesh: dom: 32 (over z, y, core), serve: 4 (over x).
Axes of the slice: x: 4, y: 4, z: 4, core: 2. Of those that a mesh axis runs over, the one named last changes fastest.
Arguments:
- embedding: float32 [262144, 256], P(('dom', 'serve')), may hold values from -40 to 40
- edge_blocks: bfloat16 [2048, 8, 128, 128], P(('dom', 'serve')), may hold values from -0.5 to 0.5
- adjacency: int32 [2048, 8], replicated, may hold values from 0 to 2047, as said below
- degrees: int32 [2048], replicated, may hold values from 2 to 8
- hash_ids: int32 [1024, 1], P('dom'), may hold values from 0 to 3; in each aligned block of 8 rows (0 to 7, 8 to 15, ...) at most 4 rows name the same one
- candidates: int32 [1024, 4], P('dom'), may hold values from 0 to 31
- head_weights: bfloat16 [4, 256, 256], replicated, may hold values from -4 to 4
Outputs:
- refreshed: float32 [262144, 256], P(('dom', 'serve'))
- task_scores: float32 [4, 2048, 128], P(None, ('dom', 'serve'))
Inputs may be any that keep to these rules, and one draw needn't show every extreme that they name: `adjacency`: A block's neighbours are item blocks if it is a user block and user blocks if it is an item block; the 8 neighbours of one block lie on 8 different devices; all neighbour slots of one device's blocks name blocks of any one device at most 1 times, and some device exactly 1 times. `hash_ids`: among the 8 user blocks of one device no shard is named more than 4 times, a bound that some block reaches.
All inputs are finite; a program needn't handle non-finite values.
Results may differ from a plain program's by a relative error of at most 0.0022.
Values may be sent and summed in bfloat16 or wider, within the bound.
No kernel may reach another device: no remote copies, remote signals or barrier semaphores. Data moves between devices by JAX's collectives and lax.ppermute only.
A program may use at most 128 MiB of HBM per device.

v0:
```python
import math

import jax
import jax.numpy as jnp
from jax import lax
from jax.sharding import PartitionSpec as P


def on_device(embedding, edge_blocks, adjacency, degrees, hash_ids, candidates, head_weights):
    blocks_dev, neighbours, block_rows, _ = edge_blocks.shape
    feature_width = embedding.shape[1]
    devices = lax.axis_size(("dom", "serve"))
    serve_count = lax.axis_size("serve")
    my_index = lax.axis_index(("dom", "serve"))
    slot_count = blocks_dev * neighbours
    capacity = max(1, slot_count // devices)
    all_lists = adjacency.reshape(devices, slot_count)
    owners = all_lists // blocks_dev
    local_ids = all_lists % blocks_dev
    from_me = (owners == my_index).astype(jnp.int32)
    send_rank = jnp.cumsum(from_me, axis=1) - 1
    rank_values = jnp.arange(capacity, dtype=jnp.int32)
    chosen = from_me[:, None, :] * (send_rank[:, None, :] == rank_values[None, :, None]).astype(
        jnp.int32
    )
    send_local = jnp.sum(chosen * local_ids[:, None, :], axis=2).reshape(devices * capacity)
    my_lists = lax.dynamic_slice_in_dim(adjacency, my_index * blocks_dev, blocks_dev, 0)
    my_owner = (my_lists // blocks_dev).reshape(slot_count)
    owner_hot = (my_owner[:, None] == jnp.arange(devices, dtype=jnp.int32)[None, :]).astype(
        jnp.int32
    )
    owner_rank = jnp.sum((jnp.cumsum(owner_hot, axis=0) - owner_hot) * owner_hot, axis=1)
    arrive_pos = my_owner * capacity + owner_rank
    degree_float = degrees.astype(jnp.float32)
    own_degree = lax.dynamic_slice_in_dim(degree_float, my_index * blocks_dev, blocks_dev, 0)
    normalizer = 1.0 / jnp.sqrt(own_degree[:, None] * jnp.take(degree_float, my_lists, axis=0))

    def propagate(layer_input):
        source_blocks = layer_input.astype(jnp.bfloat16).reshape(
            blocks_dev, block_rows, feature_width
        )
        outgoing = jnp.take(source_blocks, send_local, axis=0)
        arrived = lax.all_to_all(
            outgoing, ("dom", "serve"), split_axis=0, concat_axis=0, tiled=True
        )
        fetched = jnp.take(arrived, arrive_pos, axis=0).reshape(
            blocks_dev, neighbours, block_rows, feature_width
        )
        products = jnp.einsum(
            "bkij,bkjd->bkid", edge_blocks, fetched, preferred_element_type=jnp.float32
        )
        summed = jnp.sum(products * normalizer[:, :, None, None], axis=1)
        return summed.reshape(blocks_dev * block_rows, feature_width)

    first = propagate(embedding)
    second = propagate(first)
    refreshed = (embedding + first + second) / 3.0
    final_blocks = refreshed.astype(jnp.bfloat16).reshape(blocks_dev, block_rows, feature_width)
    user_half = blocks_dev // 2
    slot_caps = blocks_dev // 4
    user_blocks = final_blocks[:user_half]
    item_blocks = final_blocks[user_half:]
    my_serve = lax.axis_index("serve")
    group_hash = hash_ids[:, 0].reshape(serve_count, user_half)
    shard_hot = (
        group_hash[:, :, None] == jnp.arange(serve_count, dtype=jnp.int32)[None, None, :]
    ).astype(jnp.int32)
    group_rank = jnp.sum((jnp.cumsum(shard_hot, axis=1) - shard_hot) * shard_hot, axis=2)
    slot_values = jnp.arange(slot_caps, dtype=jnp.int32)
    user_local = jnp.arange(user_half, dtype=jnp.int32)
    own_hash = jnp.take(group_hash, my_serve, axis=0)
    own_rank = jnp.take(group_rank, my_serve, axis=0)
    target_pick = (
        (own_hash[None, None, :] == jnp.arange(serve_count, dtype=jnp.int32)[:, None, None])
        & (own_rank[None, None, :] == slot_values[None, :, None])
    ).astype(jnp.int32)
    send_users = jnp.sum(target_pick * user_local[None, None, :], axis=2).reshape(
        serve_count * slot_caps
    )
    leaving = jnp.take(user_blocks, send_users, axis=0).reshape(
        serve_count, slot_caps, block_rows, feature_width
    )
    landed = lax.all_to_all(leaving, "serve", split_axis=0, concat_axis=0, tiled=True)
    served = jnp.einsum(
        "scrd,kde->sckre", landed, head_weights, preferred_element_type=jnp.float32
    ).astype(jnp.bfloat16)
    gathered = lax.all_gather(item_blocks, "serve", axis=0, tiled=True)
    arrive_pick = (
        (group_hash[:, None, :] == my_serve)
        & (group_rank[:, None, :] == slot_values[None, :, None])
    ).astype(jnp.int32)
    slot_valid = jnp.sum(arrive_pick, axis=2).astype(jnp.float32)
    group_cands = candidates.reshape(serve_count, user_half, candidates.shape[1])
    slot_cands = jnp.sum(arrive_pick[:, :, :, None] * group_cands[:, None, :, :], axis=2)
    scale = 1.0 / math.sqrt(feature_width)

    def score(operands):
        projection, cand_ids, validity = operands
        item_rows = jnp.take(gathered, cand_ids, axis=0).reshape(-1, feature_width)
        affinity = (
            jnp.einsum("kre,ne->krn", projection, item_rows, preferred_element_type=jnp.float32)
            * scale
        )
        return jnp.mean(jax.nn.sigmoid(affinity), axis=2) * validity

    slot_total = serve_count * slot_caps
    results = lax.map(
        score,
        (
            served.reshape(slot_total, served.shape[2], block_rows, feature_width),
            slot_cands.reshape(slot_total, slot_cands.shape[2]),
            slot_valid.reshape(slot_total),
        ),
    )
    return (refreshed, jnp.moveaxis(results, 0, 1))


def solution(mesh):
    placed = (
        P(("dom", "serve"), None),
        P(("dom", "serve"), None, None, None),
        P(),
        P(),
        P("dom", None),
        P("dom", None),
        P(),
    )
    return jax.shard_map(
        on_device,
        mesh=mesh,
        in_specs=placed,
        out_specs=(P(("dom", "serve"), None), P(None, ("dom", "serve"), None)),
        check_vma=False,
    )
```

profile of v0, /device:TPU:0, one launch (start us, length us, event | category | flops | bytes accessed | tf_op | source)
XLA Modules:
  0.0 473.5 jit_solution(14277744058519669404)
XLA Ops:
  11.5 1.7 convert_element_type.49
  13.2 6.5 %gather_fusion.3 = bf16[128,128,256]{2,1,0:T(8,128)(2,1)} fusion(bf16[16,128,256]{2,1,0:T(8,128)(2,1)S(1)} %bitcast.81, s32[1024]{0:T(1024)S(1)} %pad_clamp_fusion.4), kind=kCustom, calls=%fused_computation.clone | custom fusion | bytes 16777728 | tf_op jit(solution)/shard_map/jit(_take)/gather | solution.py:42
  19.7 7.4 %broadcast_select_fusion.4 = bf16[128,128,256]{2,1,0:T(8,128)(2,1)} fusion(bf16[128,128,256]{2,1,0:T(8,128)(2,1)} %gather_fusion.3, pred[128]{0:T(512)(128)(4,1)S(1)} %compare_and_fusion.2), kind=kLoop, calls=%fused_computation.29 | loop fusion | flops 4194304 | bytes 16777344 | tf_op jit(solution)/shard_map/jit(_take)/select_n | solution.py:42
  27.1 11.9 %all-to-all-start = ((bf16[128,128,256]{2,1,0:T(8,128)(2,1)}), bf16[128,128,256]{2,1,0:T(8,128)(2,1)}, u32[]{:S(2)}, u32[]{:S(2)}) async-start(bf16[128,128,256]{2,1,0:T(8,128)(2,1)} %broadcast_select_fusion.4), calls=%async_computation | async-start | bytes 16777216 | tf_op jit(solution)/shard_map/all_to_all | solution.py:43
  41.1 100.0 %all-to-all-done = bf16[128,128,256]{2,1,0:T(8,128)(2,1)} async-done(((bf16[128,128,256]{2,1,0:T(8,128)(2,1)}), bf16[128,128,256]{2,1,0:T(8,128)(2,1)}, u32[]{:S(2)}, u32[]{:S(2)}) %all-to-all-start) | async-done | bytes 8388640 | tf_op jit(solution)/shard_map/all_to_all | solution.py:43
  141.1 9.9 %gather_fusion.4 = bf16[128,128,256]{2,1,0:T(8,128)(2,1)} fusion(bf16[128,128,256]{2,1,0:T(8,128)(2,1)} %all-to-all-done, s32[1024]{0:T(1024)S(1)} %pad_clamp_fusion.3), kind=kCustom, calls=%fused_computation.1.clone | custom fusion | bytes 16777728 | tf_op jit(solution)/shard_map/jit(_take)/gather | solution.py:46
  151.0 7.4 %broadcast_select_fusion.3 = bf16[128,128,256]{2,1,0:T(8,128)(2,1)} fusion(bf16[128,128,256]{2,1,0:T(8,128)(2,1)} %gather_fusion.4, pred[128]{0:T(512)(128)(4,1)S(1)} %get-tuple-element.93), kind=kLoop, calls=%fused_computation.28 | loop fusion | flops 4194304 | bytes 16777344 | tf_op jit(solution)/shard_map/jit(_take)/select_n | solution.py:46
  158.4 9.8 %multiply_reduce_fusion.1 = f32[16,256,128]{2,1,0:T(8,128)S(1)} fusion(bf16[16,8,128,256]{3,2,1,0:T(8,128)(2,1)} %bitcast.83, bf16[16,8,128,128]{3,2,1,0:T(8,128)(2,1)} %param.16, f32[16,8]{1,0:T(8,128)S(1)} %multiply_rsqrt_fusion), kind=kOutput, calls=%fused_computation.25 | convolution fusion | flops 1081606144 | bytes 14680576 | tf_op jit(solution)/shard_map/bkij,bkjd->bkid/dot_general | solution.py:49
  169.8 6.5 %gather_fusion.5 = bf16[128,128,256]{1,2,0:T(8,128)(2,1)} fusion(bf16[16,128,256]{1,2,0:T(8,128)(2,1)S(1)} %bitcast_convert_fusion, s32[1024]{0:T(1024)S(1)} %pad_clamp_fusion.4), kind=kCustom, calls=%fused_computation.3.clone | custom fusion | bytes 16777728 | tf_op jit(solution)/shard_map/jit(_take)/gather | solution.py:42
  176.3 7.4 %broadcast_select_fusion.2 = bf16[128,128,256]{1,2,0:T(8,128)(2,1)} fusion(bf16[128,128,256]{1,2,0:T(8,128)(2,1)} %gather_fusion.5, pred[128]{0:T(512)(128)(4,1)S(1)} %compare_and_fusion.2), kind=kLoop, calls=%fused_computation.27 | loop fusion | flops 4194304 | bytes 16777344 | tf_op jit(solution)/shard_map/jit(_take)/select_n | solution.py:42
  183.7 6.1 %all-to-all-start.1 = ((bf16[128,128,256]{1,2,0:T(8,128)(2,1)}), bf16[128,128,256]{1,2,0:T(8,128)(2,1)}, u32[]{:S(2)}, u32[]{:S(2)}) async-start(bf16[128,128,256]{1,2,0:T(8,128)(2,1)} %broadcast_select_fusion.2), calls=%async_computation.1 | async-start | bytes 16777216 | tf_op jit(solution)/shard_map/all_to_all | solution.py:43
  190.1 1.9 copy.67
  191.9 100.1 %all-to-all-done.1 = bf16[128,128,256]{1,2,0:T(8,128)(2,1)} async-done(((bf16[128,128,256]{1,2,0:T(8,128)(2,1)}), bf16[128,128,256]{1,2,0:T(8,128)(2,1)}, u32[]{:S(2)}, u32[]{:S(2)}) %all-to-all-start.1) | async-done | bytes 8388640 | tf_op jit(solution)/shard_map/all_to_all | solution.py:43
  292.0 9.9 %gather_fusion.6 = bf16[128,128,256]{1,2,0:T(8,128)(2,1)} fusion(bf16[128,128,256]{1,2,0:T(8,128)(2,1)} %all-to-all-done.1, s32[1024]{0:T(1024)S(1)} %pad_clamp_fusion.3), kind=kCustom, calls=%fused_computation.4.clone | custom fusion | bytes 16777728 | tf_op jit(solution)/shard_map/jit(_take)/gather | solution.py:46
  302.0 7.4 %broadcast_select_fusion.1 = bf16[128,128,256]{1,2,0:T(8,128)(2,1)} fusion(bf16[128,128,256]{1,2,0:T(8,128)(2,1)} %gather_fusion.6, pred[128]{0:T(512)(128)(4,1)S(1)} %get-tuple-element.93), kind=kLoop, calls=%fused_computation.26 | loop fusion | flops 4194304 | bytes 16777344 | tf_op jit(solution)/shard_map/jit(_take)/select_n | solution.py:46
  309.4 8.5 %multiply_reduce_fusion = f32[16,256,128]{2,1,0:T(8,128)} fusion(bf16[16,8,128,256]{2,3,1,0:T(8,128)(2,1)} %bitcast.82, bf16[16,8,128,128]{3,2,1,0:T(8,128)(2,1)} %param.16, f32[16,8]{1,0:T(8,128)S(1)} %multiply_rsqrt_fusion), kind=kOutput, calls=%fused_computation.24 | convolution fusion | flops 1081606144 | bytes 14680576 | tf_op jit(solution)/shard_map/bkij,bkjd->bkid/dot_general | solution.py:49
  317.9 3.0 copy.68
  320.9 4.0 fusion.31
  329.8 5.1 %all-to-all-start.2 = ((bf16[4,4,128,256]{3,2,1,0:T(8,128)(2,1)}), bf16[4,4,128,256]{3,2,1,0:T(8,128)(2,1)S(1)}, u32[]{:S(2)}, u32[]{:S(2)}) async-start(bf16[4,4,128,256]{3,2,1,0:T(8,128)(2,1)} %broadcast_select_fusion.5), calls=%async_computation.2 | async-start | bytes 2097152 | tf_op jit(solution)/shard_map/all_to_all | solution.py:83
  335.6 26.4 %all-to-all-done.2 = bf16[4,4,128,256]{3,2,1,0:T(8,128)(2,1)S(1)} async-done(((bf16[4,4,128,256]{3,2,1,0:T(8,128)(2,1)}), bf16[4,4,128,256]{3,2,1,0:T(8,128)(2,1)S(1)}, u32[]{:S(2)}, u32[]{:S(2)}) %all-to-all-start.2) | async-done | bytes 1048608 | tf_op jit(solution)/shard_map/all_to_all | solution.py:83
  362.1 3.2 convolution_convert_fusion
  365.2 101.4 %while.11 = (s32[]{:T(128)}, f32[16,4,128]{2,0,1:T(8,128)}, bf16[16,4,128,256]{3,2,1,0:T(8,128)(2,1)}, s32[16,4]{1,0:T(8,128)S(1)}, bf16[32,128,256]{2,1,0:T(8,1...) while((s32[]{:T(128)}, f32[16,4,128]{2,0,1:T(8,128)}, ...), condition=%wide.region_14.18_spmd, body=%wide.region_12.17_spmd.sunk | while | flops 135660576 | bytes 1587933 | solution.py:107
  365.3 2.2 gather_fusion
  367.5 1.5 fusion.46
  370.2 1.3 dynamic_update_slice.5
  371.6 2.2 gather_fusion
  373.9 1.5 fusion.46
  376.6 1.3 dynamic_update_slice.5
  377.9 2.2 gather_fusion
  380.2 1.5 fusion.46
  382.9 1.3 dynamic_update_slice.5
  384.3 2.2 gather_fusion
  386.6 1.5 fusion.46
  389.2 1.3 dynamic_update_slice.5
  390.6 2.2 gather_fusion
  392.9 1.5 fusion.46
  395.6 1.3 dynamic_update_slice.5
  396.9 2.2 gather_fusion
  399.2 1.5 fusion.46
  401.9 1.3 dynamic_update_slice.5
  403.3 2.2 gather_fusion
  405.6 1.5 fusion.46
  408.3 1.3 dynamic_update_slice.5
  409.6 2.2 gather_fusion
  411.9 1.5 fusion.46
  414.6 1.3 dynamic_update_slice.5
  416.0 2.2 gather_fusion
  418.2 1.5 fusion.46
  422.3 2.2 gather_fusion
  424.6 1.5 fusion.46
  427.3 1.3 dynamic_update_slice.5
  428.6 2.2 gather_fusion
  430.9 1.5 fusion.46
  433.6 1.3 dynamic_update_slice.5
  435.0 2.2 gather_fusion
  437.2 1.5 fusion.46
  441.3 2.2 gather_fusion
  443.6 1.5 fusion.46
  447.6 2.2 gather_fusion
  449.9 1.5 fusion.46
  454.0 2.2 gather_fusion
  456.3 1.5 fusion.46
  460.3 2.2 gather_fusion
  462.6 1.5 fusion.46
  (174 shorter events, 33.3 us)
Async XLA Ops:
  7.2 354.9 %copy-start = (bf16[4,256,256]{2,1,0:T(8,128)(2,1)S(1)}, bf16[4,256,256]{2,1,0:T(8,128)(2,1)}, u32[]{:S(2)}) copy-start(bf16[4,256,256]{2,1,0:T(8,128)(2,1)} %param.21) | copy-start | bytes 1572868
  27.1 12.3 %copy-start.4 = (s32[2048]{0:T(1024)S(1)}, s32[2048]{0:T(1024)}, u32[]{:S(2)}) copy-start(s32[2048]{0:T(1024)} %param.18) | copy-start | bytes 24580
  27.1 114.0 %all-to-all-start = ((bf16[128,128,256]{2,1,0:T(8,128)(2,1)}), bf16[128,128,256]{2,1,0:T(8,128)(2,1)}, u32[]{:S(2)}, u32[]{:S(2)}) async-start(bf16[128,128,256]{2,1,0:T(8,128)(2,1)} %broadcast_select_fusion.4), calls=%async_computation | async-start | bytes 16777216 | tf_op jit(solution)/shard_map/all_to_all | solution.py:43
  168.3 1.3 copy-start.1
  183.7 6.3 %copy-start.2 = (f32[16,256,128]{2,1,0:T(8,128)S(1)}, f32[16,256,128]{2,1,0:T(8,128)}, u32[]{:S(2)}) copy-start(f32[16,256,128]{2,1,0:T(8,128)} %copy-done.1) | copy-start | bytes 6291460
  183.7 108.3 %all-to-all-start.1 = ((bf16[128,128,256]{1,2,0:T(8,128)(2,1)}), bf16[128,128,256]{1,2,0:T(8,128)(2,1)}, u32[]{:S(2)}, u32[]{:S(2)}) async-start(bf16[128,128,256]{1,2,0:T(8,128)(2,1)} %broadcast_select_fusion.2), calls=%async_computation.1 | async-start | bytes 16777216 | tf_op jit(solution)/shard_map/all_to_all | solution.py:43
  189.8 175.4 %all-gather.2.cloned.1.call-start = ((), (), s32[]{:S(2)}) async-start(), calls=%async_computation.3 | async-start | bytes 2621440 | tf_op jit(solution)/shard_map/all_gather | solution.py:87
  309.4 11.5 %copy-start.3 = (f32[2048,256]{1,0:T(8,128)S(1)}, f32[2048,256]{1,0:T(8,128)}, u32[]{:S(2)}) copy-start(f32[2048,256]{1,0:T(8,128)} %param.15) | copy-start | bytes 6291460
  317.9 8.3 %copy-start.6 = (s32[32,1]{0,1:T(1,128)S(1)}, s32[32,1]{0,1:T(1,128)}, u32[]{:S(2)}) copy-start(s32[32,1]{0,1:T(1,128)} %param.19) | copy-start | bytes 388
  320.9 14.0 %copy-start.5 = (s32[32,4]{0,1:T(4,128)S(1)}, s32[32,4]{0,1:T(4,128)}, u32[]{:S(2)}) copy-start(s32[32,4]{0,1:T(4,128)} %param.20) | copy-start | bytes 1540
  329.8 32.2 %all-to-all-start.2 = ((bf16[4,4,128,256]{3,2,1,0:T(8,128)(2,1)}), bf16[4,4,128,256]{3,2,1,0:T(8,128)(2,1)S(1)}, u32[]{:S(2)}, u32[]{:S(2)}) async-start(bf16[4,4,128,256]{3,2,1,0:T(8,128)(2,1)} %broadcast_select_fusion.5), calls=%async_computation.2 | async-start | bytes 2097152 | tf_op jit(solution)/shard_map/all_to_all | solution.py:83
Sparse Core Ops, SparseCore 0:
  325.8 39.0 all-gather.1
where the time goes:
time: 477 us; the launch traced here: 473 us
  waiting for transfers between devices  227 us (48%)
  local copies, waits for them, and re-layouts  111 us (23%)
  matrix products  45.6 us (10%)
  other arithmetic  43 us (9%)
  starting transfers between devices  23.2 us (5%)
  between operations  14.3 us (3%)
  loops' own time  9.71 us (2%)
    all_to_all x2, waiting for transfers between devices, propagate(): lax.all_to_all(outgoing, ('dom', 'serve'), split_axis=0, concat_axis=0, t...  200 us
    gather x16, local copies, waits for them, and re-layouts, score(): item_rows = jnp.take(gathered, cand_ids, axis=0).reshape(-1, feature_width)  34.4 us
    all_to_all x1, waiting for transfers between devices, on_device(): lax.all_to_all(leaving, 'serve', split_axis=0, concat_axis=0, tiled=True)  26.4 us
    dot_general x16, matrix products, score(): jnp.einsum('kre,ne->krn', projection, item_rows, preferred_element_type=j...  24.1 us
    dynamic_update_slice x16, local copies, waits for them, and re-layouts, on_device(): lax.map(score, (served.reshape(slot_total, served.shape[2], block_rows, f...  21.5 us
    gather x2, local copies, waits for them, and re-layouts, propagate(): jnp.take(arrived, arrive_pos, axis=0)  19.9 us
    dot_general x2, matrix products, propagate(): jnp.einsum('bkij,bkjd->bkid', edge_blocks, fetched, preferred_element_typ...  18.3 us
    all_to_all x2, starting transfers between devices, propagate(): lax.all_to_all(outgoing, ('dom', 'serve'), split_axis=0, concat_axis=0, t...  17.9 us
  transfers between devices with their start and end apart: 4, of which 3 were waited for; matrix products, arithmetic and copies ran while one was open for 3% of the time, Pallas kernels for 0%

commit v1 on v0

v1 whole, which is shorter than its diff:
```python
import functools
import math

import jax
import jax.numpy as jnp
from jax import lax
from jax.experimental import pallas as pl
from jax.experimental.pallas import tpu as pltpu
from jax.sharding import Mesh, PartitionSpec as P

AXES = ("z", "y", "core", "x")
SIZES = (4, 4, 2, 4)
DOM = ("z", "y", "core")
ORDER = ("z", "x", "y", "core")

BLOCKS = 16
HALF = 8
NEAR = 8
ROWS = 128
WIDTH = 256
DEVICES = 128
NBLK = DEVICES * BLOCKS
TASKS = 4
CANDS = 4
SERVE = 4
CAPS = 4
BF16 = jnp.bfloat16
F32 = jnp.float32
ANY = pl.BlockSpec(memory_space=pl.ANY)
SMEM = pl.BlockSpec(memory_space=pltpu.SMEM)
VMEM = pl.BlockSpec(memory_space=pltpu.VMEM)
DMA = pltpu.SemaphoreType.DMA


def params(mib):
    return pltpu.CompilerParams(vmem_limit_bytes=mib * 1024 * 1024)


def cost(flops, mib, transcendentals=0):
    return pl.CostEstimate(
        flops=flops, bytes_accessed=mib * 1024 * 1024, transcendentals=transcendentals
    )


def place_of(device):
    coords, rest = {}, device
    for axis, size in reversed(list(zip(AXES, SIZES))):
        coords[axis] = rest % size
        rest = rest // size
    place = 0
    for axis in ORDER:
        place = place * SIZES[AXES.index(axis)] + coords[axis]
    return place


PLACES = [place_of(device) for device in range(DEVICES)]


def first_kernel(adj_ref, x_ref, out_ref, loc_ref, held, found, found_smem, sem):
    me = lax.axis_index(AXES)
    adj = adj_ref[...]
    hits = jnp.where(adj // BLOCKS == me, adj % BLOCKS, 0)
    for step in (1, 2, 4, 8):
        hits = hits + pltpu.roll(hits, NBLK - step, 1)
    found[...] = jnp.sum(hits, axis=0, keepdims=True)
    copy = pltpu.make_async_copy(found, found_smem, sem)
    copy.start()
    held[...] = x_ref[...].astype(BF16)
    copy.wait()
    for device, place in enumerate(PLACES):
        block = found_smem[0, device * BLOCKS]
        loc_ref[place] = block
        out_ref[place] = held[block]


def first_messages(adjacency, embedding):
    return pl.pallas_call(
        first_kernel,
        in_specs=[VMEM, VMEM],
        out_specs=[VMEM, SMEM],
        out_shape=[
            pltpu.VMEM((DEVICES, ROWS, WIDTH), BF16),
            jax.ShapeDtypeStruct((DEVICES,), jnp.int32),
        ],
        scratch_shapes=[
            pltpu.VMEM((BLOCKS, ROWS, WIDTH), BF16),
            pltpu.VMEM((1, NBLK), jnp.int32),
            pltpu.SMEM((1, NBLK), jnp.int32),
            DMA,
        ],
        compiler_params=params(8),
        cost_estimate=cost(0, 10),
        name="first_messages",
    )(adjacency, embedding)


def load_lists(adj_hbm, lists, sem):
    me = lax.axis_index(AXES)
    window = pl.ds(pl.multiple_of(me // NEAR * ROWS, ROWS), ROWS)
    copy = pltpu.make_async_copy(adj_hbm.at[:, window], lists, sem)
    copy.start()
    copy.wait()
    return me


def gathered_sum(me, g, lists, degree_ref, edge_ref, arrived_ref):
    own = degree_ref[me * BLOCKS + g]
    total = None
    for k in range(NEAR):
        far = lists[k, me % NEAR * BLOCKS + g]
        degree = (own * degree_ref[far]).astype(F32)
        product = jnp.dot(
            edge_ref[g, k], arrived_ref[place_of(far // BLOCKS)], preferred_element_type=F32
        )
        product = product * (1.0 / jnp.sqrt(jnp.full((1, WIDTH), degree)))
        total = product if total is None else total + product
    return total


def layer_one_kernel(
    loc_ref, degree_ref, adj_hbm, edge_ref, arrived_ref, e1_ref, out_ref, held, lists, sem
):
    me = load_lists(adj_hbm, lists, sem)

    def step(g, carry):
        total = gathered_sum(me, g, lists, degree_ref, edge_ref, arrived_ref)
        e1_ref[g] = total
        held[g] = total.astype(BF16)
        return carry

    lax.fori_loop(0, BLOCKS, step, 0)

    def send(q, carry):
        out_ref[q] = held[loc_ref[q]]
        return carry

    lax.fori_loop(0, DEVICES, send, 0, unroll=4)


def layer_one(loc, degrees, adjacency, edge_blocks, arrived):
    return pl.pallas_call(
        layer_one_kernel,
        in_specs=[SMEM, SMEM, ANY, VMEM, VMEM],
        out_specs=[VMEM, VMEM],
        out_shape=[
            pltpu.VMEM((BLOCKS, ROWS, WIDTH), F32),
            pltpu.VMEM((DEVICES, ROWS, WIDTH), BF16),
        ],
        scratch_shapes=[
            pltpu.VMEM((BLOCKS, ROWS, WIDTH), BF16),
            pltpu.SMEM((NEAR, ROWS), jnp.int32),
            DMA,
        ],
        compiler_params=params(8),
        cost_estimate=cost(2 * BLOCKS * NEAR * ROWS * ROWS * WIDTH, 22),
        name="layer_one",
    )(loc, degrees, adjacency, edge_blocks, arrived)


def layer_two_kernel(*refs, base, project):
    degree_ref, adj_hbm, edge_ref, arrived_ref, e0_ref, e1_ref = refs[:6]
    if project:
        weight_ref, _, refreshed_hbm, final_ref = refs[6:10]
    else:
        refreshed_hbm, final_ref = refs[6:8]
    refreshed, lists, sem, out_sem = refs[-4:]
    me = load_lists(adj_hbm, lists, sem)

    def step(i, carry):
        g = base + i
        total = gathered_sum(me, g, lists, degree_ref, edge_ref, arrived_ref)
        value = (e0_ref[g] + e1_ref[g] + total) / 3.0
        refreshed[i] = value
        pltpu.make_async_copy(refreshed.at[i], refreshed_hbm.at[g], out_sem).start()
        rows = value.astype(BF16)
        if project:
            for t in range(TASKS):
                z = jnp.dot(rows, weight_ref[t], preferred_element_type=F32).astype(BF16)
                final_ref[i, t * ROWS : (t + 1) * ROWS] = z * (0.5 / math.sqrt(WIDTH))
        else:
            final_ref[i] = rows
        return carry

    lax.fori_loop(0, HALF, step, 0)
    pltpu.make_async_copy(refreshed, refreshed, out_sem).wait()


def layer_two(
    degrees, adjacency, edge_blocks, arrived, embedding, e1, base, weights=None, refreshed=None
):
    project = weights is not None
    in_specs = [SMEM, ANY, VMEM, VMEM, VMEM, VMEM]
    operands = [degrees, adjacency, edge_blocks, arrived, embedding, e1]
    aliases, rows = {}, ROWS
    if project:
        in_specs += [VMEM, ANY]
        operands += [weights, refreshed]
        aliases, rows = {7: 0}, TASKS * ROWS
    flops = 2 * HALF * ROWS * WIDTH * (NEAR * ROWS + (TASKS * WIDTH if project else 0))
    return pl.pallas_call(
        functools.partial(layer_two_kernel, base=base, project=project),
        in_specs=in_specs,
        out_specs=[ANY, VMEM],
        out_shape=[
            jax.ShapeDtypeStruct((BLOCKS, ROWS, WIDTH), F32),
            pltpu.VMEM((HALF, rows, WIDTH), BF16),
        ],
        scratch_shapes=[
            pltpu.VMEM((HALF, ROWS, WIDTH), F32),
            pltpu.SMEM((NEAR, ROWS), jnp.int32),
            DMA,
            DMA,
        ],
        input_output_aliases=aliases,
        compiler_params=params(8),
        cost_estimate=cost(flops, 10),
        name="layer_two_users" if project else "layer_two_items",
    )(*operands)


def score_kernel(hash_ref, cand_ref, z_ref, *refs):
    pieces, out_ref, items = refs[:-2], refs[-2], refs[-1]
    my_serve = lax.axis_index("x")
    at = 0
    for piece in pieces:
        size = piece.shape[0]
        items[at : at + size] = piece[...]
        at += size
    out_ref[...] = jnp.zeros_like(out_ref)

    def step(g, carry):
        user = my_serve * HALF + g
        shard = hash_ref[0, user]
        rank = jnp.int32(0)
        for other in range(HALF - 1):
            same = (hash_ref[0, my_serve * HALF + other] == shard) & (other < g)
            rank = rank + same.astype(jnp.int32)
        total = jnp.zeros((8, TASKS * ROWS), F32)
        for j in range(CANDS):
            cand = cand_ref[j, user]
            back = (my_serve - cand // HALF + SERVE) % SERVE
            affinity = lax.dot_general(
                items[back * HALF + cand % HALF],
                z_ref[g],
                (((1,), (1,)), ((), ())),
                preferred_element_type=F32,
            )
            curved = jnp.tanh(affinity).reshape(ROWS // 8, 8, TASKS * ROWS)
            total = total + jnp.sum(curved, axis=0)
        mean = 0.5 + (0.5 / (CANDS * ROWS)) * jnp.sum(total, axis=0, keepdims=True)
        for t in range(TASKS):
            out_ref[shard * CAPS + rank, t : t + 1, :] = mean[:, t * ROWS : (t + 1) * ROWS]
        return carry

    lax.fori_loop(0, HALF, step, 0)


def score(hashes, cands, z, pieces):
    count = HALF * TASKS * ROWS * CANDS * ROWS
    return pl.pallas_call(
        score_kernel,
        in_specs=[SMEM, SMEM, VMEM] + [VMEM] * len(pieces),
        out_specs=VMEM,
        out_shape=pltpu.VMEM((SERVE * CAPS, TASKS, ROWS), F32),
        scratch_shapes=[pltpu.VMEM((SERVE * HALF, ROWS, WIDTH), BF16)],
        compiler_params=params(8),
        cost_estimate=cost(2 * count * WIDTH, 5, count),
        name="score",
    )(hashes, cands, z, *pieces)


def exchange(messages):
    return lax.all_to_all(messages, ORDER, split_axis=0, concat_axis=0, tiled=True)


def shift(blocks, by):
    return lax.ppermute(blocks, "x", [(s, (s + by) % SERVE) for s in range(SERVE)])


def on_device(embedding, edge_blocks, adjacency, degrees, hash_ids, candidates, head_weights):
    blocks = embedding.reshape(BLOCKS, ROWS, WIDTH)
    lists = adjacency.T
    messages, loc = first_messages(lists, blocks)
    arrived = exchange(messages)
    e1, messages = layer_one(loc, degrees, lists, edge_blocks, arrived)
    arrived = exchange(messages)
    shared = (degrees, lists, edge_blocks, arrived, blocks, e1)
    refreshed, items = layer_two(*shared, HALF)
    pieces = [
        items,
        shift(items, 1),
        shift(items[: HALF // 2], 2),
        shift(items[HALF // 2 :], 2),
        shift(items, 3),
    ]
    refreshed, z = layer_two(*shared, 0, head_weights, refreshed)
    scores = score(hash_ids.T, candidates.T, z, pieces)
    scores = scores.reshape(SERVE, CAPS, TASKS, ROWS)
    landed = lax.all_to_all(scores, "x", split_axis=0, concat_axis=0, tiled=True)
    task_scores = jnp.moveaxis(landed.reshape(SERVE * CAPS, TASKS, ROWS), 1, 0)
    return refreshed.reshape(BLOCKS * ROWS, WIDTH), task_scores


def solution(mesh):
    fine = Mesh(mesh.devices.reshape(SIZES), AXES)
    placed = (
        P(AXES, None),
        P(AXES, None, None, None),
        P(),
        P(),
        P(DOM, None),
        P(DOM, None),
        P(),
    )
    return jax.shard_map(
        on_device,
        mesh=fine,
        in_specs=placed,
        out_specs=(P(AXES, None), P(None, AXES, None)),
        check_vma=False,
    )
```

time: 477 us -> 270 us (0.57)
  blocking collectives: 0 us -> 219 us
  waiting for transfers between devices: 227 us -> 14.3 us
  local copies, waits for them, and re-layouts: 111 us -> 3.12 us
  matrix products: 45.6 us -> 0 us
  other arithmetic: 43 us -> 0 us
  Pallas kernels: 0 us -> 27 us
  starting transfers between devices: 23.2 us -> 5.7 us
  between operations: 14.3 us -> 0.72 us
  loops' own time: 9.71 us -> 0 us
    all_to_all x3 -> x0, waiting for transfers between devices: 227 us -> none  [the longest x2 200 us: propagate(): lax.all_to_all(outgoing, ('dom', 'serve'), split_axis=0, concat_axis=0, t...]
    all_to_all x0 -> x3, blocking collectives: none -> 219 us  [the longest x2 211 us: exchange(): lax.all_to_all(messages, ORDER, split_axis=0, concat_axis=0, tiled=True)]
    gather x23 -> x0, local copies, waits for them, and re-layouts: 69.3 us -> none  [the longest x16 34.4 us: score(): item_rows = jnp.take(gathered, cand_ids, axis=0).reshape(-1, feature_width)]
    dot_general x19 -> x0, matrix products: 45.6 us -> none  [the longest x16 24.1 us: score(): jnp.einsum('kre,ne->krn', projection, item_rows, preferred_element_type=j...]
    select_n x41 -> x0, other arithmetic: 32.4 us -> none  [the longest x3 14.8 us: propagate(): outgoing = jnp.take(source_blocks, send_local, axis=0)]
    pallas_call x0 -> x5, Pallas kernels: none -> 27 us  [the longest x2 11.8 us: layer_two(): pl.pallas_call(functools.partial(layer_two_kernel, base=base, project=pro...]
    all_to_all x3 -> x0, starting transfers between devices: 23 us -> none  [the longest x2 17.9 us: propagate(): lax.all_to_all(outgoing, ('dom', 'serve'), split_axis=0, concat_axis=0, t...]
    dynamic_update_slice x16 -> x0, local copies, waits for them, and re-layouts: 21.5 us -> none  [on_device(): lax.map(score, (served.reshape(slot_total, served.shape[2], block_rows, f...]
  transfers between devices with their start and end apart: 4 -> 4, of which waited for: 3 -> 3; matrix products, arithmetic and copies ran while one was open for 3% -> 0% of each run, Pallas kernels for 0% -> 2%
where the time goes in v1:
time: 270 us
  blocking collectives  219 us (81%)
  Pallas kernels  27 us (10%)
  waiting for transfers between devices  14.3 us (5%)
  starting transfers between devices  5.7 us (2%)
  local copies, waits for them, and re-layouts  3.12 us (1%)
    all_to_all x2, blocking collectives, exchange(): lax.all_to_all(messages, ORDER, split_axis=0, concat_axis=0, tiled=True)  211 us
    ppermute x4, waiting for transfers between devices, shift(): lax.ppermute(blocks, 'x', [(s, (s + by) % SERVE) for s in range(SERVE)])  14.3 us
    pallas_call x2, Pallas kernels, layer_two(): pl.pallas_call(functools.partial(layer_two_kernel, base=base, project=pro...  11.8 us
    pallas_call x1, Pallas kernels, layer_one(): pl.pallas_call(layer_one_kernel, in_specs=[SMEM, SMEM, ANY, VMEM, VMEM],...  8.51 us
    all_to_all x1, blocking collectives, on_device(): lax.all_to_all(scores, 'x', split_axis=0, concat_axis=0, tiled=True)  8 us
    ppermute x4, starting transfers between devices, shift(): lax.ppermute(blocks, 'x', [(s, (s + by) % SERVE) for s in range(SERVE)])  5.7 us
  transfers between devices with their start and end apart: 4, of which 3 were waited for; matrix products, arithmetic and copies ran while one was open for 0% of the time, Pallas kernels for 2%

profile of v1, /device:TPU:0, one launch (start us, length us, event | category | flops | bytes accessed | tf_op | source)
XLA Modules:
  0.0 269.7 jit_solution(16024446109446532229)
XLA Ops:
  0.6 0.0 copy-start.1
  0.6 1.6 copy-done.1
  2.2 0.0 copy-start.3
  2.2 0.8 copy-done.3
  3.1 2.1 first_messages.1
  5.1 0.0 copy-start
  5.1 0.0 copy-start.6
  5.2 108.8 %all_to_all.15.arrived_ref = bf16[128,128,256]{2,1,0:T(8,128)(2,1)S(1)} all-to-all(bf16[128,128,256]{2,1,0:T(8,128)(2,1)S(1)} %get-tuple-element.11), channel_id=1, replica_groups=mesh['z'=4,'y'=4,'core'=2,'x'=4] {'z','x','y','core'}, dimensions={0} | all-to-all | bytes 16777216 | tf_op jit(solution)/shard_map/all_to_all | solution.py:273
  114.0 0.0 copy-done
  114.0 0.0 copy-done.6
  114.0 8.5 %layer_one.1 = (f32[16,128,256]{2,1,0:T(8,128)S(1)}, bf16[128,128,256]{2,1,0:T(8,128)(2,1)S(1)}) custom-call(s32[128]{0:T(128)S(1)} %get-tuple-element.10.loc_ref, s32[2048]{0:T(1024)S(1)} %copy-done.6, s32[8,2048]{1,0:T(8,128)S(1)} %bitcast.13, bf16[16,8,128,128]{3,2,1,0:T(8,128)(2,1)S(1)} %copy-done, bf16[128,128,256]{2,1,0:T(8,128)(2,1)S(1)} %all_to_all.15.arrived_ref), custom_call_target="tpu_custom_call" | custom-call | flops 1073741824 | bytes 23068672 | tf_op jit(solution)/shard_map/layer_one/pallas_call | solution.py:141
  122.5 0.0 copy-start.2
  122.5 102.0 %all_to_all.16.refs_3_ = bf16[128,128,256]{2,1,0:T(8,128)(2,1)S(1)} all-to-all(bf16[128,128,256]{2,1,0:T(8,128)(2,1)S(1)} %get-tuple-element.12), channel_id=1, replica_groups=mesh['z'=4,'y'=4,'core'=2,'x'=4] {'z','x','y','core'}, dimensions={0} | all-to-all | bytes 16777216 | tf_op jit(solution)/shard_map/all_to_all | solution.py:273
  224.5 0.0 copy-done.2
  224.5 0.0 copy-start.4
  224.5 0.0 copy-start.5
  224.6 5.2 %layer_two_items.1 = (f32[16,128,256]{2,1,0:T(8,128)}, bf16[8,128,256]{2,1,0:T(8,128)(2,1)S(1)}) custom-call(s32[2048]{0:T(1024)S(1)} %copy-done.6, s32[8,2048]{1,0:T(8,128)S(1)} %bitcast.14, bf16[16,8,128,128]{3,2,1,0:T(8,128)(2,1)S(1)} %copy-done, bf16[128,128,256]{2,1,0:T(8,128)(2,1)S(1)} %all_to_all.16.refs_3_, f32[16,128,256]{2,1,0:T(8,128)S(1)} %bitcast.10, ...), custom_call_target="tpu_custom_call" | custom-call | flops 536870912 | bytes 10485760 | tf_op jit(solution)/shard_map/layer_two_items/pallas_call | solution.py:200
  229.8 1.3 collective-permute-start.3
  231.1 0.8 collective-permute-start
  231.9 0.8 collective-permute-start.2
  232.7 2.8 %collective-permute-start.1 = (bf16[4,128,256]{2,1,0:T(8,128)(2,1)S(1)}, bf16[4,128,256]{2,1,0:T(8,128)(2,1)S(1)}, u32[]{:S(2)}, u32[]{:S(2)}) collective-permute-start(bf16[4,128,256]{2,1,0:T(8,128)(2,1)S(1)} %get-tuple-element.19), channel_id=1, source_target_pairs={{0,2},{1,3},{2,0},{3,1},{4,6},{5,7},{6,4},{7,5},{8,10},{9,11},{10,... | collective-permute-start | bytes 786440 | tf_op jit(solution)/shard_map/ppermute | solution.py:277
  235.5 0.0 copy-done.4
  235.5 0.0 copy-done.5
  235.5 0.0 copy-start.7
  235.5 0.0 copy-start.8
  235.5 6.6 %layer_two_users.1 = (f32[16,128,256]{2,1,0:T(8,128)}, bf16[8,512,256]{2,1,0:T(8,128)(2,1)S(1)}) custom-call(s32[2048]{0:T(1024)S(1)} %copy-done.6, s32[8,2048]{1,0:T(8,128)S(1)} %bitcast.15, bf16[16,8,128,128]{3,2,1,0:T(8,128)(2,1)S(1)} %copy-done, bf16[128,128,256]{2,1,0:T(8,128)(2,1)S(1)} %all_to_all.16.refs_3_, ...), custom_call_target="tpu_custom_call", output_to_operand_aliasing={{0}: (7, {})} | custom-call | flops 1073741824 | bytes 10485760 | tf_op jit(solution)/shard_map/layer_two_users/pallas_call | solution.py:200
  242.1 9.1 %collective-permute-done.2.refs_3_ = bf16[4,128,256]{2,1,0:T(8,128)(2,1)S(1)} collective-permute-done((bf16[4,128,256]{2,1,0:T(8,128)(2,1)S(1)}, bf16[4,128,256]{2,1,0:T(8,128)(2,1)S(1)}, u32[]{:S(2)}, u32[]{:S(2)}) %collective-permute-start.2) | collective-permute-done | bytes 262176 | tf_op jit(solution)/shard_map/ppermute | solution.py:277
  251.2 3.9 %collective-permute-done.1.refs_2_ = bf16[4,128,256]{2,1,0:T(8,128)(2,1)S(1)} collective-permute-done((bf16[4,128,256]{2,1,0:T(8,128)(2,1)S(1)}, bf16[4,128,256]{2,1,0:T(8,128)(2,1)S(1)}, u32[]{:S(2)}, u32[]{:S(2)}) %collective-permute-start.1) | collective-permute-done | bytes 262176 | tf_op jit(solution)/shard_map/ppermute | solution.py:277
  255.1 0.0 collective-permute-done.3.refs_4_
  255.1 1.3 collective-permute-done.refs_1_
  256.4 0.0 copy-done.7
  256.4 0.0 copy-done.8
  256.4 4.7 %score.1 = f32[16,4,128]{2,1,0:T(4,128)S(1)} custom-call(s32[1,32]{1,0:T(1,128)S(1)} %bitcast.18, s32[4,32]{1,0:T(4,128)S(1)} %bitcast.17, bf16[8,512,256]{2,1,0:T(8,128)(2,1)S(1)} %get-tuple-element.16.z_ref, bf16[8,128,256]{2,1,0:T(8,128)(2,1)S(1)} %get-tuple-element.17.refs_0_, bf16[8,128,256]{2,1,0:T(8,128)(2,1)S(1)} %collective-permute-done.refs_1_, ...), custom_call_target="tpu_custom_call" | custom-call | flops 1073741824 | bytes 5242880 | tf_op jit(solution)/shard_map/score/pallas_call | solution.py:260
  261.1 8.0 %all_to_all.17 = f32[4,4,4,128]{3,2,1,0:T(4,128)S(1)} all-to-all(f32[4,4,4,128]{3,2,1,0:T(4,128)S(1)} %bitcast.16), channel_id=1, replica_groups=mesh['z'=4,'y'=4,'core'=2,'x'=4] {'x'}, dimensions={0} | all-to-all | bytes 65536 | tf_op jit(solution)/shard_map/all_to_all | solution.py:299
  269.1 0.6 copy.10
  (1 shorter events, 0.0 us)
Async XLA Ops:
  0.6 1.6 copy-start.1
  2.2 0.8 copy-start.3
  5.1 108.9 %copy-start = (bf16[16,8,128,128]{3,2,1,0:T(8,128)(2,1)S(1)}, bf16[16,8,128,128]{3,2,1,0:T(8,128)(2,1)}, u32[]{:S(2)}) copy-start(bf16[16,8,128,128]{3,2,1,0:T(8,128)(2,1)} %refs_2_.3) | copy-start | bytes 12582916
  5.1 108.8 %copy-start.6 = (s32[2048]{0:T(1024)S(1)}, s32[2048]{0:T(1024)}, u32[]{:S(2)}) copy-start(s32[2048]{0:T(1024)} %refs_0_.3) | copy-start | bytes 24580
  122.5 102.0 %copy-start.2 = (f32[2048,256]{1,0:T(8,128)S(1)}, f32[2048,256]{1,0:T(8,128)}, u32[]{:S(2)}) copy-start(f32[2048,256]{1,0:T(8,128)} %param.7) | copy-start | bytes 6291460
  224.5 11.0 %copy-start.4 = (s32[2048,8]{0,1:T(8,128)S(1)}, s32[2048,8]{0,1:T(8,128)}, u32[]{:S(2)}) copy-start(s32[2048,8]{0,1:T(8,128)} %param.9) | copy-start | bytes 196612
  224.5 11.0 %copy-start.5 = (bf16[4,256,256]{2,1,0:T(8,128)(2,1)S(1)}, bf16[4,256,256]{2,1,0:T(8,128)(2,1)}, u32[]{:S(2)}) copy-start(bf16[4,256,256]{2,1,0:T(8,128)(2,1)} %refs_6_.1) | copy-start | bytes 1572868
  229.8 25.3 %collective-permute-start.3 = (bf16[8,128,256]{2,1,0:T(8,128)(2,1)S(1)}, bf16[8,128,256]{2,1,0:T(8,128)(2,1)S(1)}, u32[]{:S(2)}, u32[]{:S(2)}) collective-permute-start(bf16[8,128,256]{2,1,0:T(8,128)(2,1)S(1)} %get-tuple-element.17.refs_0_), channel_id=1, source_target_pairs={{0,3},{1,0},{2,1},{3,2},{4,7},{5,4},{6,5},{7,6},{8,11},{9,8},{10,9... | collective-permute-start | bytes 1572872 | tf_op jit(solution)/shard_map/ppermute | solution.py:277
  231.1 25.3 %collective-permute-start = (bf16[8,128,256]{2,1,0:T(8,128)(2,1)S(1)}, bf16[8,128,256]{2,1,0:T(8,128)(2,1)S(1)}, u32[]{:S(2)}, u32[]{:S(2)}) collective-permute-start(bf16[8,128,256]{2,1,0:T(8,128)(2,1)S(1)} %get-tuple-element.17.refs_0_), channel_id=1, source_target_pairs={{0,1},{1,2},{2,3},{3,0},{4,5},{5,6},{6,7},{7,4},{8,9},{9,10},{10,1... | collective-permute-start | bytes 1572872 | tf_op jit(solution)/shard_map/ppermute | solution.py:277
  231.9 19.3 %collective-permute-start.2 = (bf16[4,128,256]{2,1,0:T(8,128)(2,1)S(1)}, bf16[4,128,256]{2,1,0:T(8,128)(2,1)S(1)}, u32[]{:S(2)}, u32[]{:S(2)}) collective-permute-start(bf16[4,128,256]{2,1,0:T(8,128)(2,1)S(1)} %get-tuple-element.18), channel_id=1, source_target_pairs={{0,2},{1,3},{2,0},{3,1},{4,6},{5,7},{6,4},{7,5},{8,10},{9,11},{10,... | collective-permute-start | bytes 786440 | tf_op jit(solution)/shard_map/ppermute | solution.py:277
  232.7 22.3 %collective-permute-start.1 = (bf16[4,128,256]{2,1,0:T(8,128)(2,1)S(1)}, bf16[4,128,256]{2,1,0:T(8,128)(2,1)S(1)}, u32[]{:S(2)}, u32[]{:S(2)}) collective-permute-start(bf16[4,128,256]{2,1,0:T(8,128)(2,1)S(1)} %get-tuple-element.19), channel_id=1, source_target_pairs={{0,2},{1,3},{2,0},{3,1},{4,6},{5,7},{6,4},{7,5},{8,10},{9,11},{10,... | collective-permute-start | bytes 786440 | tf_op jit(solution)/shard_map/ppermute | solution.py:277
  235.5 20.9 %copy-start.7 = (s32[32,4]{0,1:T(4,128)S(1)}, s32[32,4]{0,1:T(4,128)}, u32[]{:S(2)}) copy-start(s32[32,4]{0,1:T(4,128)} %param.12) | copy-start | bytes 1540
  235.5 20.9 %copy-start.8 = (s32[32,1]{0,1:T(1,128)S(1)}, s32[32,1]{0,1:T(1,128)}, u32[]{:S(2)}) copy-start(s32[32,1]{0,1:T(1,128)} %param.11) | copy-start | bytes 388

commit v2 on v1

v2 whole, which is shorter than its diff:
```python
import functools
import math

import jax
import jax.numpy as jnp
from jax import lax
from jax.experimental import pallas as pl
from jax.experimental.pallas import tpu as pltpu
from jax.sharding import Mesh, PartitionSpec as P

AXES = ("z", "y", "core", "x")
SIZES = (4, 4, 2, 4)
DOM = ("z", "y", "core")
ORDER = ("z", "x", "y", "core")

BLOCKS = 16
HALF = 8
PIECE = 4
NEAR = 8
ROWS = 128
WIDTH = 256
DEVICES = 128
NBLK = DEVICES * BLOCKS
LANES = 128
LINES = NBLK // LANES
TASKS = 4
CANDS = 4
SERVE = 4
CAPS = 4
BF16 = jnp.bfloat16
F32 = jnp.float32
ANY = pl.BlockSpec(memory_space=pl.ANY)
SMEM = pl.BlockSpec(memory_space=pltpu.SMEM)
VMEM = pl.BlockSpec(memory_space=pltpu.VMEM)
DMA = pltpu.SemaphoreType.DMA


def params(mib):
    return pltpu.CompilerParams(vmem_limit_bytes=mib * 1024 * 1024)


def cost(flops, mib, transcendentals=0):
    return pl.CostEstimate(
        flops=flops, bytes_accessed=mib * 1024 * 1024, transcendentals=transcendentals
    )


def place_of(device):
    coords, rest = {}, device
    for axis, size in reversed(list(zip(AXES, SIZES))):
        coords[axis] = rest % size
        rest = rest // size
    place = 0
    for axis in ORDER:
        place = place * SIZES[AXES.index(axis)] + coords[axis]
    return place


PLACES = [place_of(device) for device in range(DEVICES)]


def first_kernel(
    adj_hbm, degree_hbm, x_hbm, out_ref, plan_ref,
    adj, degrees, x, held, plan, adj_sem, degree_sem, x_sem, plan_sem,
):
    me = lax.axis_index(AXES)
    adj_copy = pltpu.make_async_copy(adj_hbm, adj, adj_sem)
    adj_copy.start()
    degree_copy = pltpu.make_async_copy(degree_hbm, degrees, degree_sem)
    degree_copy.start()
    x_copies = [
        pltpu.make_async_copy(x_hbm.at[pl.ds(i, PIECE)], x.at[pl.ds(i, PIECE)], x_sem.at[i // PIECE])
        for i in range(0, BLOCKS, PIECE)
    ]
    for copy in x_copies:
        copy.start()

    adj_copy.wait()
    listed = adj[...]
    hits = jnp.where(listed // BLOCKS == me, listed % BLOCKS, 0)
    for step in (1, 2, 4, 8):
        hits = hits + pltpu.roll(hits, NBLK - step, 1)
    hits = jnp.sum(hits, axis=0, keepdims=True)
    for i in range(LINES):
        plan_ref[i : i + 1] = hits[:, i * LANES : (i + 1) * LANES]

    degree_copy.wait()
    mine = adj[:, pl.ds(pl.multiple_of(me // NEAR * LANES, LANES), LANES)]
    far = jnp.zeros_like(mine)
    for i in range(LINES):
        line = jnp.broadcast_to(degrees[i : i + 1], mine.shape)
        line = jnp.take_along_axis(line, mine % LANES, axis=1, mode="promise_in_bounds")
        far = jnp.where(mine // LANES == i, line, far)
    own = degrees[pl.ds(me // NEAR, 1)]
    plan_ref[LINES:] = place_of(mine // BLOCKS) + far * own * DEVICES

    plan_copy = pltpu.make_async_copy(plan_ref, plan, plan_sem)
    plan_copy.start()
    for i, copy in enumerate(x_copies):
        copy.wait()
        piece = slice(i * PIECE, (i + 1) * PIECE)
        held[piece] = x[piece].astype(BF16)
    plan_copy.wait()
    send(plan, held, out_ref)


def send(plan, held, out_ref):
    for device, place in enumerate(PLACES):
        at = device * BLOCKS
        out_ref[place] = held[plan[at // LANES, at % LANES]]


def first_messages(adjacency, degrees, embedding):
    return pl.pallas_call(
        first_kernel,
        in_specs=[ANY, ANY, ANY],
        out_specs=[VMEM, VMEM],
        out_shape=[
            pltpu.VMEM((DEVICES, ROWS, WIDTH), BF16),
            pltpu.VMEM((LINES + NEAR, LANES), jnp.int32),
        ],
        scratch_shapes=[
            pltpu.VMEM((NEAR, NBLK), jnp.int32),
            pltpu.VMEM((LINES, LANES), jnp.int32),
            pltpu.VMEM((BLOCKS, ROWS, WIDTH), F32),
            pltpu.VMEM((BLOCKS, ROWS, WIDTH), BF16),
            pltpu.SMEM((LINES + NEAR, LANES), jnp.int32),
            DMA,
            DMA,
            DMA((BLOCKS // PIECE,)),
            DMA,
        ],
        compiler_params=params(8),
        cost_estimate=cost(0, 10),
        name="first_messages",
    )(*[pltpu.with_memory_space_constraint(a, pltpu.HBM) for a in (adjacency, degrees, embedding)])


def gathered_sum(g, plan_ref, edge_ref, arrived_ref):
    column = lax.axis_index(AXES) % NEAR * BLOCKS + g
    total = None
    for k in range(NEAR):
        word = plan_ref[LINES + k, column]
        degree = (word // DEVICES).astype(F32)
        product = jnp.dot(
            edge_ref[g, k], arrived_ref[word % DEVICES], preferred_element_type=F32
        )
        product = product * (1.0 / jnp.sqrt(jnp.full((1, WIDTH), degree)))
        total = product if total is None else total + product
    return total


def layer_one_kernel(plan_ref, edge_ref, arrived_ref, e1_ref, out_ref, held):
    for g in range(BLOCKS):
        total = gathered_sum(g, plan_ref, edge_ref, arrived_ref)
        e1_ref[g] = total
        held[g] = total.astype(BF16)

    send(plan_ref, held, out_ref)


def layer_one(plan, edge_blocks, arrived):
    return pl.pallas_call(
        layer_one_kernel,
        in_specs=[SMEM, VMEM, VMEM],
        out_specs=[VMEM, VMEM],
        out_shape=[
            pltpu.VMEM((BLOCKS, ROWS, WIDTH), F32),
            pltpu.VMEM((DEVICES, ROWS, WIDTH), BF16),
        ],
        scratch_shapes=[pltpu.VMEM((BLOCKS, ROWS, WIDTH), BF16)],
        compiler_params=params(8),
        cost_estimate=cost(2 * BLOCKS * NEAR * ROWS * ROWS * WIDTH, 22),
        name="layer_one",
    )(plan, edge_blocks, arrived)


def items_kernel(plan_ref, edge_ref, arrived_ref, e0_ref, e1_ref, refreshed_ref, *final_refs):
    for i in range(HALF):
        g = HALF + i
        total = gathered_sum(g, plan_ref, edge_ref, arrived_ref)
        value = (e0_ref[g] + e1_ref[g] + total) / 3.0
        refreshed_ref[i] = value
        final_refs[i // PIECE][i % PIECE] = value.astype(BF16)


def layer_two_items(plan, *arrays):
    return pl.pallas_call(
        items_kernel,
        in_specs=[SMEM] + [VMEM] * 4,
        out_specs=[VMEM] * 3,
        out_shape=[pltpu.VMEM((HALF, ROWS, WIDTH), F32)]
        + [pltpu.VMEM((PIECE, ROWS, WIDTH), BF16)] * 2,
        compiler_params=params(8),
        cost_estimate=cost(2 * HALF * ROWS * WIDTH * NEAR * ROWS, 10),
        name="layer_two_items",
    )(plan, *arrays)


def users_kernel(
    plan_ref, edge_ref, arrived_ref, e0_ref, e1_ref, weight_ref, items_ref, out_hbm, z_ref,
    users, user_sem, item_sem,
):
    item_copy = pltpu.make_async_copy(items_ref, out_hbm.at[pl.ds(HALF, HALF)], item_sem)
    item_copy.start()
    for g in range(HALF):
        total = gathered_sum(g, plan_ref, edge_ref, arrived_ref)
        value = (e0_ref[g] + e1_ref[g] + total) / 3.0
        users[g] = value
        rows = value.astype(BF16)
        for t in range(TASKS):
            z = jnp.dot(rows, weight_ref[t], preferred_element_type=F32).astype(BF16)
            z_ref[g, t * ROWS : (t + 1) * ROWS] = z * (0.5 / math.sqrt(WIDTH))
    user_copy = pltpu.make_async_copy(users, out_hbm.at[pl.ds(0, HALF)], user_sem)
    user_copy.start()
    item_copy.wait()
    user_copy.wait()


def layer_two_users(plan, *arrays):
    flops = 2 * HALF * ROWS * WIDTH * (NEAR * ROWS + TASKS * WIDTH)
    return pl.pallas_call(
        users_kernel,
        in_specs=[SMEM] + [VMEM] * 6,
        out_specs=[ANY, VMEM],
        out_shape=[
            jax.ShapeDtypeStruct((BLOCKS, ROWS, WIDTH), F32),
            pltpu.VMEM((HALF, TASKS * ROWS, WIDTH), BF16),
        ],
        scratch_shapes=[pltpu.VMEM((HALF, ROWS, WIDTH), F32), DMA, DMA],
        compiler_params=params(8),
        cost_estimate=cost(flops, 10),
        name="layer_two_users",
    )(plan, *arrays)


def score_kernel(hash_ref, cand_ref, z_ref, *refs):
    pieces, out_ref, items = refs[:-2], refs[-2], refs[-1]
    my_serve = lax.axis_index("x")
    at = 0
    for piece in pieces:
        size = piece.shape[0]
        items[at : at + size] = piece[...]
        at += size
    out_ref[...] = jnp.zeros_like(out_ref)

    def step(g, carry):
        user = my_serve * HALF + g
        shard = hash_ref[0, user]
        rank = jnp.int32(0)
        for other in range(HALF - 1):
            same = (hash_ref[0, my_serve * HALF + other] == shard) & (other < g)
            rank = rank + same.astype(jnp.int32)
        rows = []
        for j in range(CANDS):
            cand = cand_ref[j, user]
            back = (my_serve - cand // HALF + SERVE) % SERVE
            rows.append(items[back * HALF + cand % HALF])
        affinity = lax.dot_general(
            jnp.concatenate(rows, axis=0),
            z_ref[g],
            (((1,), (1,)), ((), ())),
            preferred_element_type=F32,
        )
        total = jnp.sum(jnp.tanh(affinity), axis=0, keepdims=True)
        mean = 0.5 + (0.5 / (CANDS * ROWS)) * total
        for t in range(TASKS):
            out_ref[shard * CAPS + rank, t : t + 1, :] = mean[:, t * ROWS : (t + 1) * ROWS]
        return carry

    lax.fori_loop(0, HALF, step, 0, unroll=2)


def score(hashes, cands, z, pieces):
    count = HALF * TASKS * ROWS * CANDS * ROWS
    return pl.pallas_call(
        score_kernel,
        in_specs=[SMEM, SMEM, VMEM] + [VMEM] * len(pieces),
        out_specs=VMEM,
        out_shape=pltpu.VMEM((SERVE * CAPS, TASKS, ROWS), F32),
        scratch_shapes=[pltpu.VMEM((SERVE * HALF, ROWS, WIDTH), BF16)],
        compiler_params=params(8),
        cost_estimate=cost(2 * count * WIDTH, 5, count),
        name="score",
    )(hashes, cands, z, *pieces)


def exchange(messages):
    return lax.all_to_all(messages, ORDER, split_axis=0, concat_axis=0, tiled=True)


def shift(blocks, by):
    return lax.ppermute(blocks, "x", [(s, (s + by) % SERVE) for s in range(SERVE)])


def on_device(embedding, edge_blocks, adjacency, degrees, hash_ids, candidates, head_weights):
    blocks = embedding.reshape(BLOCKS, ROWS, WIDTH)
    messages, plan = first_messages(adjacency.T, degrees.reshape(LINES, LANES), blocks)
    arrived = exchange(messages)
    e1, messages = layer_one(plan, edge_blocks, arrived)
    arrived = exchange(messages)
    shared = (plan, edge_blocks, arrived, blocks, e1)
    refreshed, items_a, items_b = layer_two_items(*shared)
    left_a, right_b = shift(items_a, 1), shift(items_b, 3)
    left_b, right_a = shift(items_b, 1), shift(items_a, 3)
    refreshed, z = layer_two_users(*shared, head_weights, refreshed)
    left_a, right_b, z = lax.optimization_barrier((left_a, right_b, z))
    far_a, far_b = shift(left_a, 1), shift(right_b, 3)
    pieces = [items_a, items_b, left_a, left_b, far_a, far_b, right_a, right_b]
    scores = score(hash_ids.T, candidates.T, z, pieces)
    scores = scores.reshape(SERVE, CAPS, TASKS, ROWS)
    landed = lax.all_to_all(scores, "x", split_axis=0, concat_axis=0, tiled=True)
    task_scores = jnp.moveaxis(landed.reshape(SERVE * CAPS, TASKS, ROWS), 1, 0)
    return refreshed.reshape(BLOCKS * ROWS, WIDTH), task_scores


def solution(mesh):
    fine = Mesh(mesh.devices.reshape(SIZES), AXES)
    placed = (
        P(AXES, None),
        P(AXES, None, None, None),
        P(),
        P(),
        P(DOM, None),
        P(DOM, None),
        P(),
    )
    return jax.shard_map(
        on_device,
        mesh=fine,
        in_specs=placed,
        out_specs=(P(AXES, None), P(None, AXES, None)),
        check_vma=False,
    )
```

time: 270 us -> 254 us (0.941)
  Pallas kernels: 27 us -> 16 us
  waiting for transfers between devices: 14.3 us -> 7.21 us
  starting transfers between devices: 5.7 us -> 8.6 us
    pallas_call x4, Pallas kernels: 22.3 us -> 13.4 us  [the longest x1 4.58 us: layer_two_users(): pl.pallas_call(users_kernel, in_specs=[SMEM] + [VMEM] * 6, out_specs=[ANY...]
    ppermute x4 -> x6, waiting for transfers between devices: 14.3 us -> 7.21 us  [shift(): lax.ppermute(blocks, 'x', [(s, (s + by) % SERVE) for s in range(SERVE)])]
    ppermute x4 -> x6, starting transfers between devices: 5.7 us -> 8.6 us  [shift(): lax.ppermute(blocks, 'x', [(s, (s + by) % SERVE) for s in range(SERVE)])]
  transfers between devices with their start and end apart: 4 -> 6, of which waited for: 3 -> 4; matrix products, arithmetic and copies ran while one was open for 0% -> 0% of each run, Pallas kernels for 2% -> 2%
where the time goes in v2:
time: 254 us; the launch traced here: 253 us
  blocking collectives  220 us (87%)
  Pallas kernels  16 us (6%)
  starting transfers between devices  8.6 us (3%)
  waiting for transfers between devices  7.21 us (3%)
    all_to_all x2, blocking collectives, exchange(): lax.all_to_all(messages, ORDER, split_axis=0, concat_axis=0, tiled=True)  211 us
    all_to_all x1, blocking collectives, on_device(): lax.all_to_all(scores, 'x', split_axis=0, concat_axis=0, tiled=True)  9.46 us
    ppermute x6, starting transfers between devices, shift(): lax.ppermute(blocks, 'x', [(s, (s + by) % SERVE) for s in range(SERVE)])  8.6 us
    ppermute x6, waiting for transfers between devices, shift(): lax.ppermute(blocks, 'x', [(s, (s + by) % SERVE) for s in range(SERVE)])  7.21 us
  transfers between devices with their start and end apart: 6, of which 4 were waited for; matrix products, arithmetic and copies ran while one was open for 0% of the time, Pallas kernels for 2%

profile of v2, /device:TPU:0, one launch (start us, length us, event | category | flops | bytes accessed | tf_op | source)
XLA Modules:
  0.0 253.5 jit_solution(9107902902301076879)
XLA Ops:
  0.6 3.1 %first_messages.1 = (bf16[128,128,256]{2,1,0:T(8,128)(2,1)S(1)}, s32[24,128]{1,0:T(8,128)S(1)}) custom-call(s32[8,2048]{1,0:T(8,128)} %bitcast.16, s32[16,128]{1,0:T(8,128)} %bitcast.18, f32[16,128,256]{2,1,0:T(8,128)} %bitcast.10), custom_call_target="tpu_custom_call" | custom-call | bytes 10485760 | tf_op jit(solution)/shard_map/first_messages/pallas_call | solution.py:114
  3.7 0.0 copy-start
  3.7 108.8 %all_to_all.15.arrived_ref = bf16[128,128,256]{2,1,0:T(8,128)(2,1)S(1)} all-to-all(bf16[128,128,256]{2,1,0:T(8,128)(2,1)S(1)} %get-tuple-element.15), channel_id=1, replica_groups=mesh['z'=4,'y'=4,'core'=2,'x'=4] {'z','x','y','core'}, dimensions={0} | all-to-all | bytes 16777216 | tf_op jit(solution)/shard_map/all_to_all | solution.py:289
  112.6 0.0 copy-done
  112.6 3.6 %layer_one.1 = (f32[16,128,256]{2,1,0:T(8,128)S(1)}, bf16[128,128,256]{2,1,0:T(8,128)(2,1)S(1)}) custom-call(s32[24,128]{1,0:T(8,128)S(1)} %get-tuple-element.14.plan_ref, bf16[16,8,128,128]{3,2,1,0:T(8,128)(2,1)S(1)} %copy-done, bf16[128,128,256]{2,1,0:T(8,128)(2,1)S(1)} %all_to_all.15.arrived_ref), custom_call_target="tpu_custom_call" | custom-call | flops 1073741824 | bytes 23068672 | tf_op jit(solution)/shard_map/layer_one/pallas_call | solution.py:163
  116.2 0.0 copy-start.1
  116.2 102.0 %all_to_all.16.arrived_ref = bf16[128,128,256]{2,1,0:T(8,128)(2,1)S(1)} all-to-all(bf16[128,128,256]{2,1,0:T(8,128)(2,1)S(1)} %get-tuple-element.16), channel_id=1, replica_groups=mesh['z'=4,'y'=4,'core'=2,'x'=4] {'z','x','y','core'}, dimensions={0} | all-to-all | bytes 16777216 | tf_op jit(solution)/shard_map/all_to_all | solution.py:289
  218.3 0.0 copy-done.1
  218.3 0.0 copy-start.2
  218.3 2.0 layer_two_items.1
  220.3 0.6 collective-permute-start
  220.9 2.7 %collective-permute-start.1 = (bf16[4,128,256]{2,1,0:T(8,128)(2,1)S(1)}, bf16[4,128,256]{2,1,0:T(8,128)(2,1)S(1)}, u32[]{:S(2)}, u32[]{:S(2)}) collective-permute-start(bf16[4,128,256]{2,1,0:T(8,128)(2,1)S(1)} %get-tuple-element.21.refs_1_), channel_id=1, source_target_pairs={{0,3},{1,0},{2,1},{3,2},{4,7},{5,4},{6,5},{7,6},{8,11},{9,8},{10,9... | collective-permute-start | bytes 786440 | tf_op jit(solution)/shard_map/ppermute | solution.py:293
  223.6 0.0 collective-permute-start.5
  223.7 2.0 collective-permute-start.2
  225.6 0.0 copy-done.2
  225.7 0.0 copy-start.3
  225.7 0.0 copy-start.4
  225.7 4.6 %layer_two_users.1 = (f32[16,128,256]{2,1,0:T(8,128)}, bf16[8,512,256]{2,1,0:T(8,128)(2,1)S(1)}) custom-call(s32[24,128]{1,0:T(8,128)S(1)} %get-tuple-element.14.plan_ref, bf16[16,8,128,128]{3,2,1,0:T(8,128)(2,1)S(1)} %copy-done, bf16[128,128,256]{2,1,0:T(8,128)(2,1)S(1)} %all_to_all.16.arrived_ref, f32[16,128,256]{2,1,0:T(8,128)S(1)} %bitcast.12, ...), custom_call_target="tpu_custom_call" | custom-call | flops 1073741824 | bytes 10485760 | tf_op jit(solution)/shard_map/layer_two_users/pallas_call | solution.py:222
  230.2 0.6 collective-permute-done.refs_2_
  230.8 0.0 collective-permute-done.1.refs_7_
  230.8 0.0 collective-permute-start.3
  230.8 3.3 %collective-permute-start.4 = (bf16[4,128,256]{2,1,0:T(8,128)(2,1)S(1)}, bf16[4,128,256]{2,1,0:T(8,128)(2,1)S(1)}, u32[]{:S(2)}, u32[]{:S(2)}) collective-permute-start(bf16[4,128,256]{2,1,0:T(8,128)(2,1)S(1)} %collective-permute-done.1.refs_7_), channel_id=1, source_target_pairs={{0,3},{1,0},{2,1},{3,2},{4,7},{5,4},{6,5},{7,6},{8,11},{9,8},{10,9... | collective-permute-start | bytes 786440 | tf_op jit(solution)/shard_map/ppermute | solution.py:293
  234.1 1.9 collective-permute-done.5.refs_6_
  236.0 0.4 collective-permute-done.2.refs_3_
  236.4 4.3 %collective-permute-done.3.refs_4_ = bf16[4,128,256]{2,1,0:T(8,128)(2,1)S(1)} collective-permute-done((bf16[4,128,256]{2,1,0:T(8,128)(2,1)S(1)}, bf16[4,128,256]{2,1,0:T(8,128)(2,1)S(1)}, u32[]{:S(2)}, u32[]{:S(2)}) %collective-permute-start.3) | collective-permute-done | bytes 262176 | tf_op jit(solution)/shard_map/ppermute | solution.py:293
  240.7 0.0 collective-permute-done.4.refs_5_
  240.7 0.0 copy-done.3
  240.7 0.0 copy-done.4
  240.7 2.6 %score.1 = f32[16,4,128]{2,1,0:T(4,128)S(1)} custom-call(s32[1,32]{1,0:T(1,128)S(1)} %bitcast.15, s32[4,32]{1,0:T(4,128)S(1)} %bitcast.14, bf16[8,512,256]{2,1,0:T(8,128)(2,1)S(1)} %get-tuple-element.23.z_ref, bf16[4,128,256]{2,1,0:T(8,128)(2,1)S(1)} %get-tuple-element.20.refs_0_, bf16[4,128,256]{2,1,0:T(8,128)(2,1)S(1)} %get-tuple-element.21.refs_1_, ...), custom_call_target="tpu_custom_call" | custom-call | flops 1073741824 | bytes 5242880 | tf_op jit(solution)/shard_map/score/pallas_call | solution.py:276
  243.4 9.5 %all_to_all.17 = f32[4,4,4,128]{3,2,1,0:T(4,128)S(1)} all-to-all(f32[4,4,4,128]{3,2,1,0:T(4,128)S(1)} %bitcast.13), channel_id=1, replica_groups=mesh['z'=4,'y'=4,'core'=2,'x'=4] {'x'}, dimensions={0} | all-to-all | bytes 65536 | tf_op jit(solution)/shard_map/all_to_all | solution.py:312
  252.8 0.6 copy.9
Async XLA Ops:
  3.7 108.8 %copy-start = (bf16[16,8,128,128]{3,2,1,0:T(8,128)(2,1)S(1)}, bf16[16,8,128,128]{3,2,1,0:T(8,128)(2,1)}, u32[]{:S(2)}) copy-start(bf16[16,8,128,128]{3,2,1,0:T(8,128)(2,1)} %edge_ref.5) | copy-start | bytes 12582916
  116.2 102.0 %copy-start.1 = (f32[2048,256]{1,0:T(8,128)S(1)}, f32[2048,256]{1,0:T(8,128)}, u32[]{:S(2)}) copy-start(f32[2048,256]{1,0:T(8,128)} %param.7) | copy-start | bytes 6291460
  218.3 7.4 %copy-start.2 = (bf16[4,256,256]{2,1,0:T(8,128)(2,1)S(1)}, bf16[4,256,256]{2,1,0:T(8,128)(2,1)}, u32[]{:S(2)}) copy-start(bf16[4,256,256]{2,1,0:T(8,128)(2,1)} %weight_ref.1) | copy-start | bytes 1572868
  220.3 10.5 %collective-permute-start = (bf16[4,128,256]{2,1,0:T(8,128)(2,1)S(1)}, bf16[4,128,256]{2,1,0:T(8,128)(2,1)S(1)}, u32[]{:S(2)}, u32[]{:S(2)}) collective-permute-start(bf16[4,128,256]{2,1,0:T(8,128)(2,1)S(1)} %get-tuple-element.20.refs_0_), channel_id=1, source_target_pairs={{0,1},{1,2},{2,3},{3,0},{4,5},{5,6},{6,7},{7,4},{8,9},{9,10},{10,1... | collective-permute-start | bytes 786440 | tf_op jit(solution)/shard_map/ppermute | solution.py:293
  220.9 9.9 %collective-permute-start.1 = (bf16[4,128,256]{2,1,0:T(8,128)(2,1)S(1)}, bf16[4,128,256]{2,1,0:T(8,128)(2,1)S(1)}, u32[]{:S(2)}, u32[]{:S(2)}) collective-permute-start(bf16[4,128,256]{2,1,0:T(8,128)(2,1)S(1)} %get-tuple-element.21.refs_1_), channel_id=1, source_target_pairs={{0,3},{1,0},{2,1},{3,2},{4,7},{5,4},{6,5},{7,6},{8,11},{9,8},{10,9... | collective-permute-start | bytes 786440 | tf_op jit(solution)/shard_map/ppermute | solution.py:293
  223.6 12.4 %collective-permute-start.5 = (bf16[4,128,256]{2,1,0:T(8,128)(2,1)S(1)}, bf16[4,128,256]{2,1,0:T(8,128)(2,1)S(1)}, u32[]{:S(2)}, u32[]{:S(2)}) collective-permute-start(bf16[4,128,256]{2,1,0:T(8,128)(2,1)S(1)} %get-tuple-element.20.refs_0_), channel_id=1, source_target_pairs={{0,3},{1,0},{2,1},{3,2},{4,7},{5,4},{6,5},{7,6},{8,11},{9,8},{10,9... | collective-permute-start | bytes 786440 | tf_op jit(solution)/shard_map/ppermute | solution.py:293
  223.7 12.8 %collective-permute-start.2 = (bf16[4,128,256]{2,1,0:T(8,128)(2,1)S(1)}, bf16[4,128,256]{2,1,0:T(8,128)(2,1)S(1)}, u32[]{:S(2)}, u32[]{:S(2)}) collective-permute-start(bf16[4,128,256]{2,1,0:T(8,128)(2,1)S(1)} %get-tuple-element.21.refs_1_), channel_id=1, source_target_pairs={{0,1},{1,2},{2,3},{3,0},{4,5},{5,6},{6,7},{7,4},{8,9},{9,10},{10,1... | collective-permute-start | bytes 786440 | tf_op jit(solution)/shard_map/ppermute | solution.py:293
  225.7 15.1 %copy-start.3 = (s32[32,4]{0,1:T(4,128)S(1)}, s32[32,4]{0,1:T(4,128)}, u32[]{:S(2)}) copy-start(s32[32,4]{0,1:T(4,128)} %param.12) | copy-start | bytes 1540
  225.7 15.1 %copy-start.4 = (s32[32,1]{0,1:T(1,128)S(1)}, s32[32,1]{0,1:T(1,128)}, u32[]{:S(2)}) copy-start(s32[32,1]{0,1:T(1,128)} %param.11) | copy-start | bytes 388
  230.8 9.9 %collective-permute-start.3 = (bf16[4,128,256]{2,1,0:T(8,128)(2,1)S(1)}, bf16[4,128,256]{2,1,0:T(8,128)(2,1)S(1)}, u32[]{:S(2)}, u32[]{:S(2)}) collective-permute-start(bf16[4,128,256]{2,1,0:T(8,128)(2,1)S(1)} %collective-permute-done.refs_2_), channel_id=1, source_target_pairs={{0,1},{1,2},{2,3},{3,0},{4,5},{5,6},{6,7},{7,4},{8,9},{9,10},{10,1... | collective-permute-start | bytes 786440 | tf_op jit(solution)/shard_map/ppermute | solution.py:293
  230.8 9.9 %collective-permute-start.4 = (bf16[4,128,256]{2,1,0:T(8,128)(2,1)S(1)}, bf16[4,128,256]{2,1,0:T(8,128)(2,1)S(1)}, u32[]{:S(2)}, u32[]{:S(2)}) collective-permute-start(bf16[4,128,256]{2,1,0:T(8,128)(2,1)S(1)} %collective-permute-done.1.refs_7_), channel_id=1, source_target_pairs={{0,3},{1,0},{2,1},{3,2},{4,7},{5,4},{6,5},{7,6},{8,11},{9,8},{10,9... | collective-permute-start | bytes 786440 | tf_op jit(solution)/shard_map/ppermute | solution.py:293

commit v3 on v2

--- a/solution.py
+++ b/solution.py
@@ -235,7 +235,7 @@
 
 
 def score_kernel(hash_ref, cand_ref, z_ref, *refs):
-    pieces, out_ref, items = refs[:-2], refs[-2], refs[-1]
+    pieces, out_refs, out_ref, items = refs[: -SERVE - 2], refs[-SERVE - 2 : -2], refs[-2], refs[-1]
     my_serve = lax.axis_index("x")
     at = 0
     for piece in pieces:
@@ -264,11 +264,14 @@
         )
         total = jnp.sum(jnp.tanh(affinity), axis=0, keepdims=True)
         mean = 0.5 + (0.5 / (CANDS * ROWS)) * total
+        slot = (shard - my_serve + SERVE) % SERVE * CAPS + rank
         for t in range(TASKS):
-            out_ref[shard * CAPS + rank, t : t + 1, :] = mean[:, t * ROWS : (t + 1) * ROWS]
+            out_ref[t, pl.ds(slot, 1), :] = mean[:, t * ROWS : (t + 1) * ROWS]
         return carry
 
-    lax.fori_loop(0, HALF, step, 0, unroll=2)
+    lax.fori_loop(0, HALF, step, 0, unroll=True)
+    for k in range(SERVE):
+        out_refs[k][...] = out_ref[:, k * CAPS : (k + 1) * CAPS, :]
 
 
 def score(hashes, cands, z, pieces):
@@ -276,13 +279,38 @@
     return pl.pallas_call(
         score_kernel,
         in_specs=[SMEM, SMEM, VMEM] + [VMEM] * len(pieces),
-        out_specs=VMEM,
-        out_shape=pltpu.VMEM((SERVE * CAPS, TASKS, ROWS), F32),
-        scratch_shapes=[pltpu.VMEM((SERVE * HALF, ROWS, WIDTH), BF16)],
+        out_specs=[VMEM] * SERVE,
+        out_shape=[pltpu.VMEM((TASKS, CAPS, ROWS), F32)] * SERVE,
+        scratch_shapes=[
+            pltpu.VMEM((TASKS, SERVE * CAPS, ROWS), F32),
+            pltpu.VMEM((SERVE * HALF, ROWS, WIDTH), BF16),
+        ],
         compiler_params=params(8),
         cost_estimate=cost(2 * count * WIDTH, 5, count),
         name="score",
     )(hashes, cands, z, *pieces)
+
+
+def collect_kernel(*refs):
+    parts, out_ref = refs[:-1], refs[-1]
+    my_serve = lax.axis_index("x")
+    values = [part[...] for part in parts]
+    for s in range(SERVE):
+        mine = values[0]
+        for k in range(1, SERVE):
+            mine = jnp.where((my_serve - s + SERVE) % SERVE == k, values[k], mine)
+        out_ref[:, s * CAPS : (s + 1) * CAPS, :] = mine
+
+
+def collect(parts):
+    return pl.pallas_call(
+        collect_kernel,
+        in_specs=[VMEM] * SERVE,
+        out_specs=VMEM,
+        out_shape=jax.ShapeDtypeStruct((TASKS, SERVE * CAPS, ROWS), F32),
+        compiler_params=params(8),
+        name="collect",
+    )(*parts)
 
 
 def exchange(messages):
@@ -307,10 +335,8 @@
     left_a, right_b, z = lax.optimization_barrier((left_a, right_b, z))
     far_a, far_b = shift(left_a, 1), shift(right_b, 3)
     pieces = [items_a, items_b, left_a, left_b, far_a, far_b, right_a, right_b]
-    scores = score(hash_ids.T, candidates.T, z, pieces)
-    scores = scores.reshape(SERVE, CAPS, TASKS, ROWS)
-    landed = lax.all_to_all(scores, "x", split_axis=0, concat_axis=0, tiled=True)
-    task_scores = jnp.moveaxis(landed.reshape(SERVE * CAPS, TASKS, ROWS), 1, 0)
+    parts = score(hash_ids.T, candidates.T, z, pieces)
+    task_scores = collect([parts[0]] + [shift(parts[k], k) for k in range(1, SERVE)])
     return refreshed.reshape(BLOCKS * ROWS, WIDTH), task_scores
 
 

time: 254 us -> 252 us (level)
  blocking collectives: 220 us -> 211 us
  starting transfers between devices: 8.6 us -> 13.1 us
  waiting for transfers between devices: 7.21 us -> 10.9 us
    all_to_all x1 -> x0, blocking collectives: 9.46 us -> none  [on_device(): lax.all_to_all(scores, 'x', split_axis=0, concat_axis=0, tiled=True)]
    ppermute x6 -> x9, starting transfers between devices: 8.6 us -> 13.1 us  [shift(): lax.ppermute(blocks, 'x', [(s, (s + by) % SERVE) for s in range(SERVE)])]
    ppermute x6 -> x9, waiting for transfers between devices: 7.21 us -> 10.9 us  [shift(): lax.ppermute(blocks, 'x', [(s, (s + by) % SERVE) for s in range(SERVE)])]
  transfers between devices with their start and end apart: 6 -> 9, of which waited for: 4 -> 7; matrix products, arithmetic and copies ran while one was open for 0% -> 0% of each run, Pallas kernels for 2% -> 2%
where the time goes in v3:
time: 252 us; the launch traced here: 251 us
  blocking collectives  211 us (84%)
  Pallas kernels  15.9 us (6%)
  starting transfers between devices  13.1 us (5%)
  waiting for transfers between devices  10.9 us (4%)
    all_to_all x2, blocking collectives, exchange(): lax.all_to_all(messages, ORDER, split_axis=0, concat_axis=0, tiled=True)  211 us
    ppermute x9, starting transfers between devices, shift(): lax.ppermute(blocks, 'x', [(s, (s + by) % SERVE) for s in range(SERVE)])  13.1 us
    ppermute x9, waiting for transfers between devices, shift(): lax.ppermute(blocks, 'x', [(s, (s + by) % SERVE) for s in range(SERVE)])  10.9 us
  transfers between devices with their start and end apart: 9, of which 7 were waited for; matrix products, arithmetic and copies ran while one was open for 0% of the time, Pallas kernels for 2%

profile of v3, /device:TPU:0, one launch (start us, length us, event | category | flops | bytes accessed | tf_op | source)
XLA Modules:
  0.0 251.5 jit_solution(6719846135932726809)
XLA Ops:
  0.6 3.1 %first_messages.1 = (bf16[128,128,256]{2,1,0:T(8,128)(2,1)S(1)}, s32[24,128]{1,0:T(8,128)S(1)}) custom-call(s32[8,2048]{1,0:T(8,128)} %bitcast.11, s32[16,128]{1,0:T(8,128)} %bitcast.12, f32[16,128,256]{2,1,0:T(8,128)} %bitcast.6), custom_call_target="tpu_custom_call" | custom-call | bytes 10485760 | tf_op jit(solution)/shard_map/first_messages/pallas_call | solution.py:114
  3.7 0.0 copy-start
  3.7 108.8 %all_to_all.10.arrived_ref = bf16[128,128,256]{2,1,0:T(8,128)(2,1)S(1)} all-to-all(bf16[128,128,256]{2,1,0:T(8,128)(2,1)S(1)} %get-tuple-element.19), channel_id=1, replica_groups=mesh['z'=4,'y'=4,'core'=2,'x'=4] {'z','x','y','core'}, dimensions={0} | all-to-all | bytes 16777216 | tf_op jit(solution)/shard_map/all_to_all | solution.py:317
  112.6 0.0 copy-done
  112.6 3.6 %layer_one.1 = (f32[16,128,256]{2,1,0:T(8,128)S(1)}, bf16[128,128,256]{2,1,0:T(8,128)(2,1)S(1)}) custom-call(s32[24,128]{1,0:T(8,128)S(1)} %get-tuple-element.18.plan_ref, bf16[16,8,128,128]{3,2,1,0:T(8,128)(2,1)S(1)} %copy-done, bf16[128,128,256]{2,1,0:T(8,128)(2,1)S(1)} %all_to_all.10.arrived_ref), custom_call_target="tpu_custom_call" | custom-call | flops 1073741824 | bytes 23068672 | tf_op jit(solution)/shard_map/layer_one/pallas_call | solution.py:163
  116.2 0.0 copy-start.1
  116.2 102.0 %all_to_all.11.arrived_ref = bf16[128,128,256]{2,1,0:T(8,128)(2,1)S(1)} all-to-all(bf16[128,128,256]{2,1,0:T(8,128)(2,1)S(1)} %get-tuple-element.20), channel_id=1, replica_groups=mesh['z'=4,'y'=4,'core'=2,'x'=4] {'z','x','y','core'}, dimensions={0} | all-to-all | bytes 16777216 | tf_op jit(solution)/shard_map/all_to_all | solution.py:317
  218.3 0.0 copy-done.1
  218.3 0.0 copy-start.2
  218.3 2.0 layer_two_items.1
  220.3 0.6 collective-permute-start
  220.9 2.7 %collective-permute-start.1 = (bf16[4,128,256]{2,1,0:T(8,128)(2,1)S(1)}, bf16[4,128,256]{2,1,0:T(8,128)(2,1)S(1)}, u32[]{:S(2)}, u32[]{:S(2)}) collective-permute-start(bf16[4,128,256]{2,1,0:T(8,128)(2,1)S(1)} %get-tuple-element.25.refs_1_), channel_id=1, source_target_pairs={{0,3},{1,0},{2,1},{3,2},{4,7},{5,4},{6,5},{7,6},{8,11},{9,8},{10,9... | collective-permute-start | bytes 786440 | tf_op jit(solution)/shard_map/ppermute | solution.py:321
  223.6 0.0 collective-permute-start.5
  223.6 2.0 collective-permute-start.2
  225.6 0.0 copy-done.2
  225.6 0.0 copy-start.3
  225.6 0.0 copy-start.4
  225.6 4.6 %layer_two_users.1 = (f32[16,128,256]{2,1,0:T(8,128)}, bf16[8,512,256]{2,1,0:T(8,128)(2,1)S(1)}) custom-call(s32[24,128]{1,0:T(8,128)S(1)} %get-tuple-element.18.plan_ref, bf16[16,8,128,128]{3,2,1,0:T(8,128)(2,1)S(1)} %copy-done, bf16[128,128,256]{2,1,0:T(8,128)(2,1)S(1)} %all_to_all.11.arrived_ref, f32[16,128,256]{2,1,0:T(8,128)S(1)} %bitcast.8, ...), custom_call_target="tpu_custom_call" | custom-call | flops 1073741824 | bytes 10485760 | tf_op jit(solution)/shard_map/layer_two_users/pallas_call | solution.py:222
  230.2 0.6 collective-permute-done.refs_2_
  230.8 0.0 collective-permute-done.1.refs_7_
  230.8 0.0 collective-permute-start.3
  230.8 3.3 %collective-permute-start.4 = (bf16[4,128,256]{2,1,0:T(8,128)(2,1)S(1)}, bf16[4,128,256]{2,1,0:T(8,128)(2,1)S(1)}, u32[]{:S(2)}, u32[]{:S(2)}) collective-permute-start(bf16[4,128,256]{2,1,0:T(8,128)(2,1)S(1)} %collective-permute-done.1.refs_7_), channel_id=1, source_target_pairs={{0,3},{1,0},{2,1},{3,2},{4,7},{5,4},{6,5},{7,6},{8,11},{9,8},{10,9... | collective-permute-start | bytes 786440 | tf_op jit(solution)/shard_map/ppermute | solution.py:321
  234.1 1.9 collective-permute-done.5.refs_6_
  236.0 0.4 collective-permute-done.2.refs_3_
  236.4 4.3 %collective-permute-done.3.refs_4_ = bf16[4,128,256]{2,1,0:T(8,128)(2,1)S(1)} collective-permute-done((bf16[4,128,256]{2,1,0:T(8,128)(2,1)S(1)}, bf16[4,128,256]{2,1,0:T(8,128)(2,1)S(1)}, u32[]{:S(2)}, u32[]{:S(2)}) %collective-permute-start.3) | collective-permute-done | bytes 262176 | tf_op jit(solution)/shard_map/ppermute | solution.py:321
  240.7 0.0 collective-permute-done.4.refs_5_
  240.7 0.0 copy-done.3
  240.7 0.0 copy-done.4
  240.7 2.0 score.1
  242.7 0.1 collective-permute-start.6
  242.8 4.4 %collective-permute-start.7 = (f32[4,4,128]{2,1,0:T(4,128)S(1)}, f32[4,4,128]{2,1,0:T(4,128)S(1)}, u32[]{:S(2)}, u32[]{:S(2)}) collective-permute-start(f32[4,4,128]{2,1,0:T(4,128)S(1)} %get-tuple-element.32), channel_id=1, source_target_pairs={{0,2},{1,3},{2,0},{3,1},{4,6},{5,7},{6,4},{7,5},{8,10},{9,11},{10,... | collective-permute-start | bytes 24584 | tf_op jit(solution)/shard_map/ppermute | solution.py:321
  247.2 0.0 collective-permute-start.8
  247.2 0.4 collective-permute-done.6.refs_1_
  247.6 1.3 collective-permute-done.7.refs_2_
  248.9 1.9 collective-permute-done.8.refs_3_
  250.8 0.6 collect.1
Async XLA Ops:
  3.7 108.8 %copy-start = (bf16[16,8,128,128]{3,2,1,0:T(8,128)(2,1)S(1)}, bf16[16,8,128,128]{3,2,1,0:T(8,128)(2,1)}, u32[]{:S(2)}) copy-start(bf16[16,8,128,128]{3,2,1,0:T(8,128)(2,1)} %edge_ref.5) | copy-start | bytes 12582916
  116.2 102.0 %copy-start.1 = (f32[2048,256]{1,0:T(8,128)S(1)}, f32[2048,256]{1,0:T(8,128)}, u32[]{:S(2)}) copy-start(f32[2048,256]{1,0:T(8,128)} %param.7) | copy-start | bytes 6291460
  218.3 7.4 %copy-start.2 = (bf16[4,256,256]{2,1,0:T(8,128)(2,1)S(1)}, bf16[4,256,256]{2,1,0:T(8,128)(2,1)}, u32[]{:S(2)}) copy-start(bf16[4,256,256]{2,1,0:T(8,128)(2,1)} %weight_ref.1) | copy-start | bytes 1572868
  220.3 10.5 %collective-permute-start = (bf16[4,128,256]{2,1,0:T(8,128)(2,1)S(1)}, bf16[4,128,256]{2,1,0:T(8,128)(2,1)S(1)}, u32[]{:S(2)}, u32[]{:S(2)}) collective-permute-start(bf16[4,128,256]{2,1,0:T(8,128)(2,1)S(1)} %get-tuple-element.24.refs_0_), channel_id=1, source_target_pairs={{0,1},{1,2},{2,3},{3,0},{4,5},{5,6},{6,7},{7,4},{8,9},{9,10},{10,1... | collective-permute-start | bytes 786440 | tf_op jit(solution)/shard_map/ppermute | solution.py:321
  220.9 9.9 %collective-permute-start.1 = (bf16[4,128,256]{2,1,0:T(8,128)(2,1)S(1)}, bf16[4,128,256]{2,1,0:T(8,128)(2,1)S(1)}, u32[]{:S(2)}, u32[]{:S(2)}) collective-permute-start(bf16[4,128,256]{2,1,0:T(8,128)(2,1)S(1)} %get-tuple-element.25.refs_1_), channel_id=1, source_target_pairs={{0,3},{1,0},{2,1},{3,2},{4,7},{5,4},{6,5},{7,6},{8,11},{9,8},{10,9... | collective-permute-start | bytes 786440 | tf_op jit(solution)/shard_map/ppermute | solution.py:321
  223.6 12.4 %collective-permute-start.5 = (bf16[4,128,256]{2,1,0:T(8,128)(2,1)S(1)}, bf16[4,128,256]{2,1,0:T(8,128)(2,1)S(1)}, u32[]{:S(2)}, u32[]{:S(2)}) collective-permute-start(bf16[4,128,256]{2,1,0:T(8,128)(2,1)S(1)} %get-tuple-element.24.refs_0_), channel_id=1, source_target_pairs={{0,3},{1,0},{2,1},{3,2},{4,7},{5,4},{6,5},{7,6},{8,11},{9,8},{10,9... | collective-permute-start | bytes 786440 | tf_op jit(solution)/shard_map/ppermute | solution.py:321
  223.6 12.8 %collective-permute-start.2 = (bf16[4,128,256]{2,1,0:T(8,128)(2,1)S(1)}, bf16[4,128,256]{2,1,0:T(8,128)(2,1)S(1)}, u32[]{:S(2)}, u32[]{:S(2)}) collective-permute-start(bf16[4,128,256]{2,1,0:T(8,128)(2,1)S(1)} %get-tuple-element.25.refs_1_), channel_id=1, source_target_pairs={{0,1},{1,2},{2,3},{3,0},{4,5},{5,6},{6,7},{7,4},{8,9},{9,10},{10,1... | collective-permute-start | bytes 786440 | tf_op jit(solution)/shard_map/ppermute | solution.py:321
  225.6 15.1 %copy-start.3 = (s32[32,4]{0,1:T(4,128)S(1)}, s32[32,4]{0,1:T(4,128)}, u32[]{:S(2)}) copy-start(s32[32,4]{0,1:T(4,128)} %param.12) | copy-start | bytes 1540
  225.6 15.1 %copy-start.4 = (s32[32,1]{0,1:T(1,128)S(1)}, s32[32,1]{0,1:T(1,128)}, u32[]{:S(2)}) copy-start(s32[32,1]{0,1:T(1,128)} %param.11) | copy-start | bytes 388
  230.8 9.9 %collective-permute-start.3 = (bf16[4,128,256]{2,1,0:T(8,128)(2,1)S(1)}, bf16[4,128,256]{2,1,0:T(8,128)(2,1)S(1)}, u32[]{:S(2)}, u32[]{:S(2)}) collective-permute-start(bf16[4,128,256]{2,1,0:T(8,128)(2,1)S(1)} %collective-permute-done.refs_2_), channel_id=1, source_target_pairs={{0,1},{1,2},{2,3},{3,0},{4,5},{5,6},{6,7},{7,4},{8,9},{9,10},{10,1... | collective-permute-start | bytes 786440 | tf_op jit(solution)/shard_map/ppermute | solution.py:321
  230.8 9.9 %collective-permute-start.4 = (bf16[4,128,256]{2,1,0:T(8,128)(2,1)S(1)}, bf16[4,128,256]{2,1,0:T(8,128)(2,1)S(1)}, u32[]{:S(2)}, u32[]{:S(2)}) collective-permute-start(bf16[4,128,256]{2,1,0:T(8,128)(2,1)S(1)} %collective-permute-done.1.refs_7_), channel_id=1, source_target_pairs={{0,3},{1,0},{2,1},{3,2},{4,7},{5,4},{6,5},{7,6},{8,11},{9,8},{10,9... | collective-permute-start | bytes 786440 | tf_op jit(solution)/shard_map/ppermute | solution.py:321
  242.7 4.9 %collective-permute-start.6 = (f32[4,4,128]{2,1,0:T(4,128)S(1)}, f32[4,4,128]{2,1,0:T(4,128)S(1)}, u32[]{:S(2)}, u32[]{:S(2)}) collective-permute-start(f32[4,4,128]{2,1,0:T(4,128)S(1)} %get-tuple-element.31), channel_id=1, source_target_pairs={{0,1},{1,2},{2,3},{3,0},{4,5},{5,6},{6,7},{7,4},{8,9},{9,10},{10,1... | collective-permute-start | bytes 24584 | tf_op jit(solution)/shard_map/ppermute | solution.py:321
  242.8 6.1 %collective-permute-start.7 = (f32[4,4,128]{2,1,0:T(4,128)S(1)}, f32[4,4,128]{2,1,0:T(4,128)S(1)}, u32[]{:S(2)}, u32[]{:S(2)}) collective-permute-start(f32[4,4,128]{2,1,0:T(4,128)S(1)} %get-tuple-element.32), channel_id=1, source_target_pairs={{0,2},{1,3},{2,0},{3,1},{4,6},{5,7},{6,4},{7,5},{8,10},{9,11},{10,... | collective-permute-start | bytes 24584 | tf_op jit(solution)/shard_map/ppermute | solution.py:321
  247.2 3.7 %collective-permute-start.8 = (f32[4,4,128]{2,1,0:T(4,128)S(1)}, f32[4,4,128]{2,1,0:T(4,128)S(1)}, u32[]{:S(2)}, u32[]{:S(2)}) collective-permute-start(f32[4,4,128]{2,1,0:T(4,128)S(1)} %get-tuple-element.33), channel_id=1, source_target_pairs={{0,3},{1,0},{2,1},{3,2},{4,7},{5,4},{6,5},{7,6},{8,11},{9,8},{10,9... | collective-permute-start | bytes 24584 | tf_op jit(solution)/shard_map/ppermute | solution.py:321

commit v4 on v3

--- a/solution.py
+++ b/solution.py
@@ -22,6 +22,8 @@
 DEVICES = 128
 NBLK = DEVICES * BLOCKS
 LANES = 128
+SHIFT = 7
+BITS = 4
 LINES = NBLK // LANES
 TASKS = 4
 CANDS = 4
@@ -77,12 +79,14 @@
 
     adj_copy.wait()
     listed = adj[...]
-    hits = jnp.where(listed // BLOCKS == me, listed % BLOCKS, 0)
+    hits = jnp.where(lax.shift_right_logical(listed, BITS) == me, listed & (BLOCKS - 1), 0)
     for step in (1, 2, 4, 8):
         hits = hits + pltpu.roll(hits, NBLK - step, 1)
     hits = jnp.sum(hits, axis=0, keepdims=True)
     for i in range(LINES):
         plan_ref[i : i + 1] = hits[:, i * LANES : (i + 1) * LANES]
+    plan_copy = pltpu.make_async_copy(plan_ref.at[pl.ds(0, LINES)], plan, plan_sem)
+    plan_copy.start()
 
     degree_copy.wait()
     mine = adj[:, pl.ds(pl.multiple_of(me // NEAR * LANES, LANES), LANES)]
@@ -94,8 +98,6 @@
     own = degrees[pl.ds(me // NEAR, 1)]
     plan_ref[LINES:] = place_of(mine // BLOCKS) + far * own * DEVICES
 
-    plan_copy = pltpu.make_async_copy(plan_ref, plan, plan_sem)
-    plan_copy.start()
     for i, copy in enumerate(x_copies):
         copy.wait()
         piece = slice(i * PIECE, (i + 1) * PIECE)
@@ -124,7 +126,7 @@
             pltpu.VMEM((LINES, LANES), jnp.int32),
             pltpu.VMEM((BLOCKS, ROWS, WIDTH), F32),
             pltpu.VMEM((BLOCKS, ROWS, WIDTH), BF16),
-            pltpu.SMEM((LINES + NEAR, LANES), jnp.int32),
+            pltpu.SMEM((LINES, LANES), jnp.int32),
             DMA,
             DMA,
             DMA((BLOCKS // PIECE,)),
@@ -136,23 +138,30 @@
     )(*[pltpu.with_memory_space_constraint(a, pltpu.HBM) for a in (adjacency, degrees, embedding)])
 
 
-def gathered_sum(g, plan_ref, edge_ref, arrived_ref):
-    column = lax.axis_index(AXES) % NEAR * BLOCKS + g
-    total = None
-    for k in range(NEAR):
-        word = plan_ref[LINES + k, column]
-        degree = (word // DEVICES).astype(F32)
-        product = jnp.dot(
-            edge_ref[g, k], arrived_ref[word % DEVICES], preferred_element_type=F32
-        )
-        product = product * (1.0 / jnp.sqrt(jnp.full((1, WIDTH), degree)))
-        total = product if total is None else total + product
-    return total
+def gathered_sums(blocks, plan_ref, edge_ref, arrived_ref):
+    first = (lax.axis_index(AXES) & (NEAR - 1)) * BLOCKS
+
+    def read(g):
+        words = [plan_ref[LINES + k, first + g] for k in range(NEAR)]
+        places = [word & (DEVICES - 1) for word in words]
+        return places, [lax.shift_right_logical(word, SHIFT).astype(F32) for word in words]
+
+    ahead = read(blocks[0])
+    for g, later in zip(blocks, list(blocks[1:]) + [None]):
+        places, degrees = ahead
+        if later is not None:
+            ahead = read(later)
+        total = None
+        for k in range(NEAR):
+            norm = 1.0 / jnp.sqrt(jnp.full((1, LANES), degrees[k]))
+            product = jnp.dot(edge_ref[g, k], arrived_ref[places[k]], preferred_element_type=F32)
+            product = product * jnp.concatenate([norm] * (WIDTH // LANES), axis=1)
+            total = product if total is None else total + product
+        yield g, total
 
 
 def layer_one_kernel(plan_ref, edge_ref, arrived_ref, e1_ref, out_ref, held):
-    for g in range(BLOCKS):
-        total = gathered_sum(g, plan_ref, edge_ref, arrived_ref)
+    for g, total in gathered_sums(range(BLOCKS), plan_ref, edge_ref, arrived_ref):
         e1_ref[g] = total
         held[g] = total.astype(BF16)
 
@@ -176,10 +185,9 @@
 
 
 def items_kernel(plan_ref, edge_ref, arrived_ref, e0_ref, e1_ref, refreshed_ref, *final_refs):
-    for i in range(HALF):
-        g = HALF + i
-        total = gathered_sum(g, plan_ref, edge_ref, arrived_ref)
-        value = (e0_ref[g] + e1_ref[g] + total) / 3.0
+    for g, total in gathered_sums(range(HALF, BLOCKS), plan_ref, edge_ref, arrived_ref):
+        i = g - HALF
+        value = (e0_ref[g] + e1_ref[g] + total) * (1.0 / 3.0)
         refreshed_ref[i] = value
         final_refs[i // PIECE][i % PIECE] = value.astype(BF16)
 
@@ -203,9 +211,8 @@
 ):
     item_copy = pltpu.make_async_copy(items_ref, out_hbm.at[pl.ds(HALF, HALF)], item_sem)
     item_copy.start()
-    for g in range(HALF):
-        total = gathered_sum(g, plan_ref, edge_ref, arrived_ref)
-        value = (e0_ref[g] + e1_ref[g] + total) / 3.0
+    for g, total in gathered_sums(range(HALF), plan_ref, edge_ref, arrived_ref):
+        value = (e0_ref[g] + e1_ref[g] + total) * (1.0 / 3.0)
         users[g] = value
         rows = value.astype(BF16)
         for t in range(TASKS):

time: 252 us -> 251 us (level)
  no operation moved by 1% of the time
where the time goes in v4:
time: 251 us
  blocking collectives  211 us (84%)
  Pallas kernels  15.7 us (6%)
  starting transfers between devices  13.1 us (5%)
  waiting for transfers between devices  10.9 us (4%)
    all_to_all x2, blocking collectives, exchange(): lax.all_to_all(messages, ORDER, split_axis=0, concat_axis=0, tiled=True)  211 us
    ppermute x9, starting transfers between devices, shift(): lax.ppermute(blocks, 'x', [(s, (s + by) % SERVE) for s in range(SERVE)])  13.1 us
    ppermute x9, waiting for transfers between devices, shift(): lax.ppermute(blocks, 'x', [(s, (s + by) % SERVE) for s in range(SERVE)])  10.9 us
  transfers between devices with their start and end apart: 9, of which 7 were waited for; matrix products, arithmetic and copies ran while one was open for 0% of the time, Pallas kernels for 2%

profile of v4, /device:TPU:0, one launch (start us, length us, event | category | flops | bytes accessed | tf_op | source)
XLA Modules:
  0.0 251.2 jit_solution(9222744391506367401)
XLA Ops:
  0.6 2.9 %first_messages.1 = (bf16[128,128,256]{2,1,0:T(8,128)(2,1)S(1)}, s32[24,128]{1,0:T(8,128)S(1)}) custom-call(s32[8,2048]{1,0:T(8,128)} %bitcast.11, s32[16,128]{1,0:T(8,128)} %bitcast.12, f32[16,128,256]{2,1,0:T(8,128)} %bitcast.6), custom_call_target="tpu_custom_call" | custom-call | bytes 10485760 | tf_op jit(solution)/shard_map/first_messages/pallas_call | solution.py:116
  3.5 0.0 copy-start
  3.5 108.8 %all_to_all.10.arrived_ref = bf16[128,128,256]{2,1,0:T(8,128)(2,1)S(1)} all-to-all(bf16[128,128,256]{2,1,0:T(8,128)(2,1)S(1)} %get-tuple-element.19), channel_id=1, replica_groups=mesh['z'=4,'y'=4,'core'=2,'x'=4] {'z','x','y','core'}, dimensions={0} | all-to-all | bytes 16777216 | tf_op jit(solution)/shard_map/all_to_all | solution.py:324
  112.4 0.0 copy-done
  112.4 3.6 %layer_one.1 = (f32[16,128,256]{2,1,0:T(8,128)S(1)}, bf16[128,128,256]{2,1,0:T(8,128)(2,1)S(1)}) custom-call(s32[24,128]{1,0:T(8,128)S(1)} %get-tuple-element.18.plan_ref, bf16[16,8,128,128]{3,2,1,0:T(8,128)(2,1)S(1)} %copy-done, bf16[128,128,256]{2,1,0:T(8,128)(2,1)S(1)} %all_to_all.10.arrived_ref), custom_call_target="tpu_custom_call" | custom-call | flops 1073741824 | bytes 23068672 | tf_op jit(solution)/shard_map/layer_one/pallas_call | solution.py:172
  116.0 0.0 copy-start.1
  116.0 102.0 %all_to_all.11.arrived_ref = bf16[128,128,256]{2,1,0:T(8,128)(2,1)S(1)} all-to-all(bf16[128,128,256]{2,1,0:T(8,128)(2,1)S(1)} %get-tuple-element.20), channel_id=1, replica_groups=mesh['z'=4,'y'=4,'core'=2,'x'=4] {'z','x','y','core'}, dimensions={0} | all-to-all | bytes 16777216 | tf_op jit(solution)/shard_map/all_to_all | solution.py:324
  218.1 0.0 copy-done.1
  218.1 0.0 copy-start.2
  218.1 2.0 layer_two_items.1
  220.1 0.6 collective-permute-start
  220.7 2.7 %collective-permute-start.1 = (bf16[4,128,256]{2,1,0:T(8,128)(2,1)S(1)}, bf16[4,128,256]{2,1,0:T(8,128)(2,1)S(1)}, u32[]{:S(2)}, u32[]{:S(2)}) collective-permute-start(bf16[4,128,256]{2,1,0:T(8,128)(2,1)S(1)} %get-tuple-element.25.refs_1_), channel_id=1, source_target_pairs={{0,3},{1,0},{2,1},{3,2},{4,7},{5,4},{6,5},{7,6},{8,11},{9,8},{10,9... | collective-permute-start | bytes 786440 | tf_op jit(solution)/shard_map/ppermute | solution.py:328
  223.4 0.0 collective-permute-start.5
  223.4 2.0 collective-permute-start.2
  225.4 0.0 copy-done.2
  225.4 0.0 copy-start.3
  225.4 0.0 copy-start.4
  225.4 4.6 %layer_two_users.1 = (f32[16,128,256]{2,1,0:T(8,128)}, bf16[8,512,256]{2,1,0:T(8,128)(2,1)S(1)}) custom-call(s32[24,128]{1,0:T(8,128)S(1)} %get-tuple-element.18.plan_ref, bf16[16,8,128,128]{3,2,1,0:T(8,128)(2,1)S(1)} %copy-done, bf16[128,128,256]{2,1,0:T(8,128)(2,1)S(1)} %all_to_all.11.arrived_ref, f32[16,128,256]{2,1,0:T(8,128)S(1)} %bitcast.8, ...), custom_call_target="tpu_custom_call" | custom-call | flops 1073741824 | bytes 10485760 | tf_op jit(solution)/shard_map/layer_two_users/pallas_call | solution.py:229
  230.0 0.6 collective-permute-done.refs_2_
  230.6 0.0 collective-permute-done.1.refs_7_
  230.6 0.0 collective-permute-start.3
  230.6 3.3 %collective-permute-start.4 = (bf16[4,128,256]{2,1,0:T(8,128)(2,1)S(1)}, bf16[4,128,256]{2,1,0:T(8,128)(2,1)S(1)}, u32[]{:S(2)}, u32[]{:S(2)}) collective-permute-start(bf16[4,128,256]{2,1,0:T(8,128)(2,1)S(1)} %collective-permute-done.1.refs_7_), channel_id=1, source_target_pairs={{0,3},{1,0},{2,1},{3,2},{4,7},{5,4},{6,5},{7,6},{8,11},{9,8},{10,9... | collective-permute-start | bytes 786440 | tf_op jit(solution)/shard_map/ppermute | solution.py:328
  233.9 1.9 collective-permute-done.5.refs_6_
  235.8 0.4 collective-permute-done.2.refs_3_
  236.2 4.3 %collective-permute-done.3.refs_4_ = bf16[4,128,256]{2,1,0:T(8,128)(2,1)S(1)} collective-permute-done((bf16[4,128,256]{2,1,0:T(8,128)(2,1)S(1)}, bf16[4,128,256]{2,1,0:T(8,128)(2,1)S(1)}, u32[]{:S(2)}, u32[]{:S(2)}) %collective-permute-start.3) | collective-permute-done | bytes 262176 | tf_op jit(solution)/shard_map/ppermute | solution.py:328
  240.5 0.0 collective-permute-done.4.refs_5_
  240.5 0.0 copy-done.3
  240.5 0.0 copy-done.4
  240.5 2.0 score.1
  242.5 0.1 collective-permute-start.6
  242.5 4.4 %collective-permute-start.7 = (f32[4,4,128]{2,1,0:T(4,128)S(1)}, f32[4,4,128]{2,1,0:T(4,128)S(1)}, u32[]{:S(2)}, u32[]{:S(2)}) collective-permute-start(f32[4,4,128]{2,1,0:T(4,128)S(1)} %get-tuple-element.32), channel_id=1, source_target_pairs={{0,2},{1,3},{2,0},{3,1},{4,6},{5,7},{6,4},{7,5},{8,10},{9,11},{10,... | collective-permute-start | bytes 24584 | tf_op jit(solution)/shard_map/ppermute | solution.py:328
  246.9 0.0 collective-permute-start.8
  246.9 0.4 collective-permute-done.6.refs_1_
  247.4 1.3 collective-permute-done.7.refs_2_
  248.7 1.9 collective-permute-done.8.refs_3_
  250.6 0.6 collect.1
Async XLA Ops:
  3.5 108.8 %copy-start = (bf16[16,8,128,128]{3,2,1,0:T(8,128)(2,1)S(1)}, bf16[16,8,128,128]{3,2,1,0:T(8,128)(2,1)}, u32[]{:S(2)}) copy-start(bf16[16,8,128,128]{3,2,1,0:T(8,128)(2,1)} %edge_ref.5) | copy-start | bytes 12582916
  116.0 102.0 %copy-start.1 = (f32[2048,256]{1,0:T(8,128)S(1)}, f32[2048,256]{1,0:T(8,128)}, u32[]{:S(2)}) copy-start(f32[2048,256]{1,0:T(8,128)} %param.7) | copy-start | bytes 6291460
  218.1 7.4 %copy-start.2 = (bf16[4,256,256]{2,1,0:T(8,128)(2,1)S(1)}, bf16[4,256,256]{2,1,0:T(8,128)(2,1)}, u32[]{:S(2)}) copy-start(bf16[4,256,256]{2,1,0:T(8,128)(2,1)} %weight_ref.1) | copy-start | bytes 1572868
  220.1 10.5 %collective-permute-start = (bf16[4,128,256]{2,1,0:T(8,128)(2,1)S(1)}, bf16[4,128,256]{2,1,0:T(8,128)(2,1)S(1)}, u32[]{:S(2)}, u32[]{:S(2)}) collective-permute-start(bf16[4,128,256]{2,1,0:T(8,128)(2,1)S(1)} %get-tuple-element.24.refs_0_), channel_id=1, source_target_pairs={{0,1},{1,2},{2,3},{3,0},{4,5},{5,6},{6,7},{7,4},{8,9},{9,10},{10,1... | collective-permute-start | bytes 786440 | tf_op jit(solution)/shard_map/ppermute | solution.py:328
  220.7 9.9 %collective-permute-start.1 = (bf16[4,128,256]{2,1,0:T(8,128)(2,1)S(1)}, bf16[4,128,256]{2,1,0:T(8,128)(2,1)S(1)}, u32[]{:S(2)}, u32[]{:S(2)}) collective-permute-start(bf16[4,128,256]{2,1,0:T(8,128)(2,1)S(1)} %get-tuple-element.25.refs_1_), channel_id=1, source_target_pairs={{0,3},{1,0},{2,1},{3,2},{4,7},{5,4},{6,5},{7,6},{8,11},{9,8},{10,9... | collective-permute-start | bytes 786440 | tf_op jit(solution)/shard_map/ppermute | solution.py:328
  223.4 12.4 %collective-permute-start.5 = (bf16[4,128,256]{2,1,0:T(8,128)(2,1)S(1)}, bf16[4,128,256]{2,1,0:T(8,128)(2,1)S(1)}, u32[]{:S(2)}, u32[]{:S(2)}) collective-permute-start(bf16[4,128,256]{2,1,0:T(8,128)(2,1)S(1)} %get-tuple-element.24.refs_0_), channel_id=1, source_target_pairs={{0,3},{1,0},{2,1},{3,2},{4,7},{5,4},{6,5},{7,6},{8,11},{9,8},{10,9... | collective-permute-start | bytes 786440 | tf_op jit(solution)/shard_map/ppermute | solution.py:328
  223.4 12.8 %collective-permute-start.2 = (bf16[4,128,256]{2,1,0:T(8,128)(2,1)S(1)}, bf16[4,128,256]{2,1,0:T(8,128)(2,1)S(1)}, u32[]{:S(2)}, u32[]{:S(2)}) collective-permute-start(bf16[4,128,256]{2,1,0:T(8,128)(2,1)S(1)} %get-tuple-element.25.refs_1_), channel_id=1, source_target_pairs={{0,1},{1,2},{2,3},{3,0},{4,5},{5,6},{6,7},{7,4},{8,9},{9,10},{10,1... | collective-permute-start | bytes 786440 | tf_op jit(solution)/shard_map/ppermute | solution.py:328
  225.4 15.1 %copy-start.3 = (s32[32,4]{0,1:T(4,128)S(1)}, s32[32,4]{0,1:T(4,128)}, u32[]{:S(2)}) copy-start(s32[32,4]{0,1:T(4,128)} %param.12) | copy-start | bytes 1540
  225.4 15.1 %copy-start.4 = (s32[32,1]{0,1:T(1,128)S(1)}, s32[32,1]{0,1:T(1,128)}, u32[]{:S(2)}) copy-start(s32[32,1]{0,1:T(1,128)} %param.11) | copy-start | bytes 388
  230.6 9.9 %collective-permute-start.3 = (bf16[4,128,256]{2,1,0:T(8,128)(2,1)S(1)}, bf16[4,128,256]{2,1,0:T(8,128)(2,1)S(1)}, u32[]{:S(2)}, u32[]{:S(2)}) collective-permute-start(bf16[4,128,256]{2,1,0:T(8,128)(2,1)S(1)} %collective-permute-done.refs_2_), channel_id=1, source_target_pairs={{0,1},{1,2},{2,3},{3,0},{4,5},{5,6},{6,7},{7,4},{8,9},{9,10},{10,1... | collective-permute-start | bytes 786440 | tf_op jit(solution)/shard_map/ppermute | solution.py:328
  230.6 9.9 %collective-permute-start.4 = (bf16[4,128,256]{2,1,0:T(8,128)(2,1)S(1)}, bf16[4,128,256]{2,1,0:T(8,128)(2,1)S(1)}, u32[]{:S(2)}, u32[]{:S(2)}) collective-permute-start(bf16[4,128,256]{2,1,0:T(8,128)(2,1)S(1)} %collective-permute-done.1.refs_7_), channel_id=1, source_target_pairs={{0,3},{1,0},{2,1},{3,2},{4,7},{5,4},{6,5},{7,6},{8,11},{9,8},{10,9... | collective-permute-start | bytes 786440 | tf_op jit(solution)/shard_map/ppermute | solution.py:328
  242.5 4.9 %collective-permute-start.6 = (f32[4,4,128]{2,1,0:T(4,128)S(1)}, f32[4,4,128]{2,1,0:T(4,128)S(1)}, u32[]{:S(2)}, u32[]{:S(2)}) collective-permute-start(f32[4,4,128]{2,1,0:T(4,128)S(1)} %get-tuple-element.31), channel_id=1, source_target_pairs={{0,1},{1,2},{2,3},{3,0},{4,5},{5,6},{6,7},{7,4},{8,9},{9,10},{10,1... | collective-permute-start | bytes 24584 | tf_op jit(solution)/shard_map/ppermute | solution.py:328
  242.5 6.1 %collective-permute-start.7 = (f32[4,4,128]{2,1,0:T(4,128)S(1)}, f32[4,4,128]{2,1,0:T(4,128)S(1)}, u32[]{:S(2)}, u32[]{:S(2)}) collective-permute-start(f32[4,4,128]{2,1,0:T(4,128)S(1)} %get-tuple-element.32), channel_id=1, source_target_pairs={{0,2},{1,3},{2,0},{3,1},{4,6},{5,7},{6,4},{7,5},{8,10},{9,11},{10,... | collective-permute-start | bytes 24584 | tf_op jit(solution)/shard_map/ppermute | solution.py:328
  246.9 3.7 %collective-permute-start.8 = (f32[4,4,128]{2,1,0:T(4,128)S(1)}, f32[4,4,128]{2,1,0:T(4,128)S(1)}, u32[]{:S(2)}, u32[]{:S(2)}) collective-permute-start(f32[4,4,128]{2,1,0:T(4,128)S(1)} %get-tuple-element.33), channel_id=1, source_target_pairs={{0,3},{1,0},{2,1},{3,2},{4,7},{5,4},{6,5},{7,6},{8,11},{9,8},{10,9... | collective-permute-start | bytes 24584 | tf_op jit(solution)/shard_map/ppermute | solution.py:328

commit v5 on v4

--- a/solution.py
+++ b/solution.py
@@ -11,7 +11,7 @@
 AXES = ("z", "y", "core", "x")
 SIZES = (4, 4, 2, 4)
 DOM = ("z", "y", "core")
-ORDER = ("z", "x", "y", "core")
+ORDER = ("z", "core", "x", "y")
 
 BLOCKS = 16
 HALF = 8

time: 251 us -> 251 us (level)
  no operation moved by 1% of the time
where the time goes in v5:
time: 251 us; the launch traced here: 250 us
  blocking collectives  209 us (83%)
  Pallas kernels  15.7 us (6%)
  starting transfers between devices  13.1 us (5%)
  waiting for transfers between devices  11.6 us (5%)
    all_to_all x2, blocking collectives, exchange(): lax.all_to_all(messages, ORDER, split_axis=0, concat_axis=0, tiled=True)  209 us
    ppermute x9, starting transfers between devices, shift(): lax.ppermute(blocks, 'x', [(s, (s + by) % SERVE) for s in range(SERVE)])  13.1 us
    ppermute x9, waiting for transfers between devices, shift(): lax.ppermute(blocks, 'x', [(s, (s + by) % SERVE) for s in range(SERVE)])  11.6 us
  transfers between devices with their start and end apart: 9, of which 7 were waited for; matrix products, arithmetic and copies ran while one was open for 0% of the time, Pallas kernels for 2%

profile of v5, /device:TPU:0, one launch (start us, length us, event | category | flops | bytes accessed | tf_op | source)
XLA Modules:
  0.0 250.4 jit_solution(4401981130031215019)
XLA Ops:
  0.6 2.9 %first_messages.1 = (bf16[128,128,256]{2,1,0:T(8,128)(2,1)S(1)}, s32[24,128]{1,0:T(8,128)S(1)}) custom-call(s32[8,2048]{1,0:T(8,128)} %bitcast.11, s32[16,128]{1,0:T(8,128)} %bitcast.12, f32[16,128,256]{2,1,0:T(8,128)} %bitcast.6), custom_call_target="tpu_custom_call" | custom-call | bytes 10485760 | tf_op jit(solution)/shard_map/first_messages/pallas_call | solution.py:116
  3.5 0.0 copy-start
  3.5 107.6 %all_to_all.10.arrived_ref = bf16[128,128,256]{2,1,0:T(8,128)(2,1)S(1)} all-to-all(bf16[128,128,256]{2,1,0:T(8,128)(2,1)S(1)} %get-tuple-element.19), channel_id=1, replica_groups=mesh['z'=4,'y'=4,'core'=2,'x'=4] {'z','core','x','y'}, dimensions={0} | all-to-all | bytes 16777216 | tf_op jit(solution)/shard_map/all_to_all | solution.py:324
  111.1 0.0 copy-done
  111.2 3.6 %layer_one.1 = (f32[16,128,256]{2,1,0:T(8,128)S(1)}, bf16[128,128,256]{2,1,0:T(8,128)(2,1)S(1)}) custom-call(s32[24,128]{1,0:T(8,128)S(1)} %get-tuple-element.18.plan_ref, bf16[16,8,128,128]{3,2,1,0:T(8,128)(2,1)S(1)} %copy-done, bf16[128,128,256]{2,1,0:T(8,128)(2,1)S(1)} %all_to_all.10.arrived_ref), custom_call_target="tpu_custom_call" | custom-call | flops 1073741824 | bytes 23068672 | tf_op jit(solution)/shard_map/layer_one/pallas_call | solution.py:172
  114.8 0.0 copy-start.1
  114.8 101.6 %all_to_all.11.arrived_ref = bf16[128,128,256]{2,1,0:T(8,128)(2,1)S(1)} all-to-all(bf16[128,128,256]{2,1,0:T(8,128)(2,1)S(1)} %get-tuple-element.20), channel_id=1, replica_groups=mesh['z'=4,'y'=4,'core'=2,'x'=4] {'z','core','x','y'}, dimensions={0} | all-to-all | bytes 16777216 | tf_op jit(solution)/shard_map/all_to_all | solution.py:324
  216.4 0.0 copy-done.1
  216.4 0.0 copy-start.2
  216.4 2.0 layer_two_items.1
  218.5 0.1 collective-permute-start
  218.6 3.2 %collective-permute-start.1 = (bf16[4,128,256]{2,1,0:T(8,128)(2,1)S(1)}, bf16[4,128,256]{2,1,0:T(8,128)(2,1)S(1)}, u32[]{:S(2)}, u32[]{:S(2)}) collective-permute-start(bf16[4,128,256]{2,1,0:T(8,128)(2,1)S(1)} %get-tuple-element.25.refs_1_), channel_id=1, source_target_pairs={{0,3},{1,0},{2,1},{3,2},{4,7},{5,4},{6,5},{7,6},{8,11},{9,8},{10,9... | collective-permute-start | bytes 786440 | tf_op jit(solution)/shard_map/ppermute | solution.py:328
  221.8 0.3 collective-permute-start.5
  222.1 1.7 collective-permute-start.2
  223.8 0.0 copy-done.2
  223.8 0.0 copy-start.3
  223.8 0.0 copy-start.4
  223.8 4.6 %layer_two_users.1 = (f32[16,128,256]{2,1,0:T(8,128)}, bf16[8,512,256]{2,1,0:T(8,128)(2,1)S(1)}) custom-call(s32[24,128]{1,0:T(8,128)S(1)} %get-tuple-element.18.plan_ref, bf16[16,8,128,128]{3,2,1,0:T(8,128)(2,1)S(1)} %copy-done, bf16[128,128,256]{2,1,0:T(8,128)(2,1)S(1)} %all_to_all.11.arrived_ref, f32[16,128,256]{2,1,0:T(8,128)S(1)} %bitcast.8, ...), custom_call_target="tpu_custom_call" | custom-call | flops 1073741824 | bytes 10485760 | tf_op jit(solution)/shard_map/layer_two_users/pallas_call | solution.py:229
  228.4 0.5 collective-permute-done.refs_2_
  228.9 0.0 collective-permute-done.1.refs_7_
  228.9 0.9 collective-permute-start.3
  229.8 2.4 collective-permute-start.4
  232.2 1.9 collective-permute-done.5.refs_6_
  234.1 0.4 collective-permute-done.2.refs_3_
  234.5 5.2 %collective-permute-done.3.refs_4_ = bf16[4,128,256]{2,1,0:T(8,128)(2,1)S(1)} collective-permute-done((bf16[4,128,256]{2,1,0:T(8,128)(2,1)S(1)}, bf16[4,128,256]{2,1,0:T(8,128)(2,1)S(1)}, u32[]{:S(2)}, u32[]{:S(2)}) %collective-permute-start.3) | collective-permute-done | bytes 262176 | tf_op jit(solution)/shard_map/ppermute | solution.py:328
  239.6 0.0 collective-permute-done.4.refs_5_
  239.7 0.0 copy-done.3
  239.7 0.0 copy-done.4
  239.7 2.0 score.1
  241.6 0.5 collective-permute-start.6
  242.1 4.0 %collective-permute-start.7 = (f32[4,4,128]{2,1,0:T(4,128)S(1)}, f32[4,4,128]{2,1,0:T(4,128)S(1)}, u32[]{:S(2)}, u32[]{:S(2)}) collective-permute-start(f32[4,4,128]{2,1,0:T(4,128)S(1)} %get-tuple-element.32), channel_id=1, source_target_pairs={{0,2},{1,3},{2,0},{3,1},{4,6},{5,7},{6,4},{7,5},{8,10},{9,11},{10,... | collective-permute-start | bytes 24584 | tf_op jit(solution)/shard_map/ppermute | solution.py:328
  246.1 0.0 collective-permute-start.8
  246.1 0.4 collective-permute-done.6.refs_1_
  246.6 1.3 collective-permute-done.7.refs_2_
  247.8 1.9 collective-permute-done.8.refs_3_
  249.8 0.6 collect.1
Async XLA Ops:
  3.5 107.6 %copy-start = (bf16[16,8,128,128]{3,2,1,0:T(8,128)(2,1)S(1)}, bf16[16,8,128,128]{3,2,1,0:T(8,128)(2,1)}, u32[]{:S(2)}) copy-start(bf16[16,8,128,128]{3,2,1,0:T(8,128)(2,1)} %edge_ref.5) | copy-start | bytes 12582916
  114.8 101.7 %copy-start.1 = (f32[2048,256]{1,0:T(8,128)S(1)}, f32[2048,256]{1,0:T(8,128)}, u32[]{:S(2)}) copy-start(f32[2048,256]{1,0:T(8,128)} %param.7) | copy-start | bytes 6291460
  216.4 7.4 %copy-start.2 = (bf16[4,256,256]{2,1,0:T(8,128)(2,1)S(1)}, bf16[4,256,256]{2,1,0:T(8,128)(2,1)}, u32[]{:S(2)}) copy-start(bf16[4,256,256]{2,1,0:T(8,128)(2,1)} %weight_ref.1) | copy-start | bytes 1572868
  218.5 10.4 %collective-permute-start = (bf16[4,128,256]{2,1,0:T(8,128)(2,1)S(1)}, bf16[4,128,256]{2,1,0:T(8,128)(2,1)S(1)}, u32[]{:S(2)}, u32[]{:S(2)}) collective-permute-start(bf16[4,128,256]{2,1,0:T(8,128)(2,1)S(1)} %get-tuple-element.24.refs_0_), channel_id=1, source_target_pairs={{0,1},{1,2},{2,3},{3,0},{4,5},{5,6},{6,7},{7,4},{8,9},{9,10},{10,1... | collective-permute-start | bytes 786440 | tf_op jit(solution)/shard_map/ppermute | solution.py:328
  218.6 10.3 %collective-permute-start.1 = (bf16[4,128,256]{2,1,0:T(8,128)(2,1)S(1)}, bf16[4,128,256]{2,1,0:T(8,128)(2,1)S(1)}, u32[]{:S(2)}, u32[]{:S(2)}) collective-permute-start(bf16[4,128,256]{2,1,0:T(8,128)(2,1)S(1)} %get-tuple-element.25.refs_1_), channel_id=1, source_target_pairs={{0,3},{1,0},{2,1},{3,2},{4,7},{5,4},{6,5},{7,6},{8,11},{9,8},{10,9... | collective-permute-start | bytes 786440 | tf_op jit(solution)/shard_map/ppermute | solution.py:328
  221.8 12.3 %collective-permute-start.5 = (bf16[4,128,256]{2,1,0:T(8,128)(2,1)S(1)}, bf16[4,128,256]{2,1,0:T(8,128)(2,1)S(1)}, u32[]{:S(2)}, u32[]{:S(2)}) collective-permute-start(bf16[4,128,256]{2,1,0:T(8,128)(2,1)S(1)} %get-tuple-element.24.refs_0_), channel_id=1, source_target_pairs={{0,3},{1,0},{2,1},{3,2},{4,7},{5,4},{6,5},{7,6},{8,11},{9,8},{10,9... | collective-permute-start | bytes 786440 | tf_op jit(solution)/shard_map/ppermute | solution.py:328
  222.1 12.4 %collective-permute-start.2 = (bf16[4,128,256]{2,1,0:T(8,128)(2,1)S(1)}, bf16[4,128,256]{2,1,0:T(8,128)(2,1)S(1)}, u32[]{:S(2)}, u32[]{:S(2)}) collective-permute-start(bf16[4,128,256]{2,1,0:T(8,128)(2,1)S(1)} %get-tuple-element.25.refs_1_), channel_id=1, source_target_pairs={{0,1},{1,2},{2,3},{3,0},{4,5},{5,6},{6,7},{7,4},{8,9},{9,10},{10,1... | collective-permute-start | bytes 786440 | tf_op jit(solution)/shard_map/ppermute | solution.py:328
  223.8 15.8 %copy-start.3 = (s32[32,4]{0,1:T(4,128)S(1)}, s32[32,4]{0,1:T(4,128)}, u32[]{:S(2)}) copy-start(s32[32,4]{0,1:T(4,128)} %param.12) | copy-start | bytes 1540
  223.8 15.8 %copy-start.4 = (s32[32,1]{0,1:T(1,128)S(1)}, s32[32,1]{0,1:T(1,128)}, u32[]{:S(2)}) copy-start(s32[32,1]{0,1:T(1,128)} %param.11) | copy-start | bytes 388
  228.9 10.8 %collective-permute-start.3 = (bf16[4,128,256]{2,1,0:T(8,128)(2,1)S(1)}, bf16[4,128,256]{2,1,0:T(8,128)(2,1)S(1)}, u32[]{:S(2)}, u32[]{:S(2)}) collective-permute-start(bf16[4,128,256]{2,1,0:T(8,128)(2,1)S(1)} %collective-permute-done.refs_2_), channel_id=1, source_target_pairs={{0,1},{1,2},{2,3},{3,0},{4,5},{5,6},{6,7},{7,4},{8,9},{9,10},{10,1... | collective-permute-start | bytes 786440 | tf_op jit(solution)/shard_map/ppermute | solution.py:328
  229.8 9.9 %collective-permute-start.4 = (bf16[4,128,256]{2,1,0:T(8,128)(2,1)S(1)}, bf16[4,128,256]{2,1,0:T(8,128)(2,1)S(1)}, u32[]{:S(2)}, u32[]{:S(2)}) collective-permute-start(bf16[4,128,256]{2,1,0:T(8,128)(2,1)S(1)} %collective-permute-done.1.refs_7_), channel_id=1, source_target_pairs={{0,3},{1,0},{2,1},{3,2},{4,7},{5,4},{6,5},{7,6},{8,11},{9,8},{10,9... | collective-permute-start | bytes 786440 | tf_op jit(solution)/shard_map/ppermute | solution.py:328
  241.6 4.9 %collective-permute-start.6 = (f32[4,4,128]{2,1,0:T(4,128)S(1)}, f32[4,4,128]{2,1,0:T(4,128)S(1)}, u32[]{:S(2)}, u32[]{:S(2)}) collective-permute-start(f32[4,4,128]{2,1,0:T(4,128)S(1)} %get-tuple-element.31), channel_id=1, source_target_pairs={{0,1},{1,2},{2,3},{3,0},{4,5},{5,6},{6,7},{7,4},{8,9},{9,10},{10,1... | collective-permute-start | bytes 24584 | tf_op jit(solution)/shard_map/ppermute | solution.py:328
  242.1 5.7 %collective-permute-start.7 = (f32[4,4,128]{2,1,0:T(4,128)S(1)}, f32[4,4,128]{2,1,0:T(4,128)S(1)}, u32[]{:S(2)}, u32[]{:S(2)}) collective-permute-start(f32[4,4,128]{2,1,0:T(4,128)S(1)} %get-tuple-element.32), channel_id=1, source_target_pairs={{0,2},{1,3},{2,0},{3,1},{4,6},{5,7},{6,4},{7,5},{8,10},{9,11},{10,... | collective-permute-start | bytes 24584 | tf_op jit(solution)/shard_map/ppermute | solution.py:328
  246.1 3.7 %collective-permute-start.8 = (f32[4,4,128]{2,1,0:T(4,128)S(1)}, f32[4,4,128]{2,1,0:T(4,128)S(1)}, u32[]{:S(2)}, u32[]{:S(2)}) collective-permute-start(f32[4,4,128]{2,1,0:T(4,128)S(1)} %get-tuple-element.33), channel_id=1, source_target_pairs={{0,3},{1,0},{2,1},{3,2},{4,7},{5,4},{6,5},{7,6},{8,11},{9,8},{10,9... | collective-permute-start | bytes 24584 | tf_op jit(solution)/shard_map/ppermute | solution.py:328

commit v6 on v5

--- a/solution.py
+++ b/solution.py
@@ -339,7 +339,6 @@
     left_a, right_b = shift(items_a, 1), shift(items_b, 3)
     left_b, right_a = shift(items_b, 1), shift(items_a, 3)
     refreshed, z = layer_two_users(*shared, head_weights, refreshed)
-    left_a, right_b, z = lax.optimization_barrier((left_a, right_b, z))
     far_a, far_b = shift(left_a, 1), shift(right_b, 3)
     pieces = [items_a, items_b, left_a, left_b, far_a, far_b, right_a, right_b]
     parts = score(hash_ids.T, candidates.T, z, pieces)

time: 251 us -> 251 us (level)
  transfers between devices with their start and end apart: 9 -> 9, of which waited for: 7 -> 5; matrix products, arithmetic and copies ran while one was open for 0% -> 0% of each run, Pallas kernels for 2% -> 2%
where the time goes in v6:
time: 251 us; the launch traced here: 250 us
  blocking collectives  209 us (83%)
  Pallas kernels  15.7 us (6%)
  starting transfers between devices  13.1 us (5%)
  waiting for transfers between devices  11.6 us (5%)
    all_to_all x2, blocking collectives, exchange(): lax.all_to_all(messages, ORDER, split_axis=0, concat_axis=0, tiled=True)  209 us
    ppermute x9, starting transfers between devices, shift(): lax.ppermute(blocks, 'x', [(s, (s + by) % SERVE) for s in range(SERVE)])  13.1 us
    ppermute x9, waiting for transfers between devices, shift(): lax.ppermute(blocks, 'x', [(s, (s + by) % SERVE) for s in range(SERVE)])  11.6 us
  transfers between devices with their start and end apart: 9, of which 5 were waited for; matrix products, arithmetic and copies ran while one was open for 0% of the time, Pallas kernels for 2%

profile of v6, /device:TPU:0, one launch (start us, length us, event | category | flops | bytes accessed | tf_op | source)
XLA Modules:
  0.0 250.4 jit_solution(17640000994839588783)
XLA Ops:
  0.6 2.9 %first_messages.1 = (bf16[128,128,256]{2,1,0:T(8,128)(2,1)S(1)}, s32[24,128]{1,0:T(8,128)S(1)}) custom-call(s32[8,2048]{1,0:T(8,128)} %bitcast.11, s32[16,128]{1,0:T(8,128)} %bitcast.12, f32[16,128,256]{2,1,0:T(8,128)} %bitcast.6), custom_call_target="tpu_custom_call" | custom-call | bytes 10485760 | tf_op jit(solution)/shard_map/first_messages/pallas_call | solution.py:116
  3.5 0.0 copy-start
  3.5 107.6 %all_to_all.10.arrived_ref = bf16[128,128,256]{2,1,0:T(8,128)(2,1)S(1)} all-to-all(bf16[128,128,256]{2,1,0:T(8,128)(2,1)S(1)} %get-tuple-element.16), channel_id=1, replica_groups=mesh['z'=4,'y'=4,'core'=2,'x'=4] {'z','core','x','y'}, dimensions={0} | all-to-all | bytes 16777216 | tf_op jit(solution)/shard_map/all_to_all | solution.py:324
  111.1 0.0 copy-done
  111.2 3.6 %layer_one.1 = (f32[16,128,256]{2,1,0:T(8,128)S(1)}, bf16[128,128,256]{2,1,0:T(8,128)(2,1)S(1)}) custom-call(s32[24,128]{1,0:T(8,128)S(1)} %get-tuple-element.15.plan_ref, bf16[16,8,128,128]{3,2,1,0:T(8,128)(2,1)S(1)} %copy-done, bf16[128,128,256]{2,1,0:T(8,128)(2,1)S(1)} %all_to_all.10.arrived_ref), custom_call_target="tpu_custom_call" | custom-call | flops 1073741824 | bytes 23068672 | tf_op jit(solution)/shard_map/layer_one/pallas_call | solution.py:172
  114.8 0.0 copy-start.1
  114.8 101.6 %all_to_all.11.arrived_ref = bf16[128,128,256]{2,1,0:T(8,128)(2,1)S(1)} all-to-all(bf16[128,128,256]{2,1,0:T(8,128)(2,1)S(1)} %get-tuple-element.17), channel_id=1, replica_groups=mesh['z'=4,'y'=4,'core'=2,'x'=4] {'z','core','x','y'}, dimensions={0} | all-to-all | bytes 16777216 | tf_op jit(solution)/shard_map/all_to_all | solution.py:324
  216.4 0.0 copy-done.1
  216.4 0.0 copy-start.2
  216.4 2.0 layer_two_items.1
  218.5 0.1 collective-permute-start
  218.6 3.2 %collective-permute-start.3 = (bf16[4,128,256]{2,1,0:T(8,128)(2,1)S(1)}, bf16[4,128,256]{2,1,0:T(8,128)(2,1)S(1)}, u32[]{:S(2)}, u32[]{:S(2)}) collective-permute-start(bf16[4,128,256]{2,1,0:T(8,128)(2,1)S(1)} %get-tuple-element.23.refs_1_), channel_id=1, source_target_pairs={{0,3},{1,0},{2,1},{3,2},{4,7},{5,4},{6,5},{7,6},{8,11},{9,8},{10,9... | collective-permute-start | bytes 786440 | tf_op jit(solution)/shard_map/ppermute | solution.py:328
  221.8 0.3 collective-permute-start.5
  222.1 1.7 collective-permute-start.1
  223.8 5.1 %collective-permute-done.refs_2_ = bf16[4,128,256]{2,1,0:T(8,128)(2,1)S(1)} collective-permute-done((bf16[4,128,256]{2,1,0:T(8,128)(2,1)S(1)}, bf16[4,128,256]{2,1,0:T(8,128)(2,1)S(1)}, u32[]{:S(2)}, u32[]{:S(2)}) %collective-permute-start) | collective-permute-done | bytes 262176 | tf_op jit(solution)/shard_map/ppermute | solution.py:328
  228.9 0.0 collective-permute-start.2
  228.9 0.0 collective-permute-done.3.refs_7_
  228.9 3.3 %collective-permute-start.4 = (bf16[4,128,256]{2,1,0:T(8,128)(2,1)S(1)}, bf16[4,128,256]{2,1,0:T(8,128)(2,1)S(1)}, u32[]{:S(2)}, u32[]{:S(2)}) collective-permute-start(bf16[4,128,256]{2,1,0:T(8,128)(2,1)S(1)} %collective-permute-done.3.refs_7_), channel_id=1, source_target_pairs={{0,3},{1,0},{2,1},{3,2},{4,7},{5,4},{6,5},{7,6},{8,11},{9,8},{10,9... | collective-permute-start | bytes 786440 | tf_op jit(solution)/shard_map/ppermute | solution.py:328
  232.1 0.0 copy-done.2
  232.2 0.0 copy-start.3
  232.2 0.0 copy-start.4
  232.2 4.6 %layer_two_users.1 = (f32[16,128,256]{2,1,0:T(8,128)}, bf16[8,512,256]{2,1,0:T(8,128)(2,1)S(1)}) custom-call(s32[24,128]{1,0:T(8,128)S(1)} %get-tuple-element.15.plan_ref, bf16[16,8,128,128]{3,2,1,0:T(8,128)(2,1)S(1)} %copy-done, bf16[128,128,256]{2,1,0:T(8,128)(2,1)S(1)} %all_to_all.11.arrived_ref, f32[16,128,256]{2,1,0:T(8,128)S(1)} %bitcast.8, ...), custom_call_target="tpu_custom_call" | custom-call | flops 1073741824 | bytes 10485760 | tf_op jit(solution)/shard_map/layer_two_users/pallas_call | solution.py:229
  236.7 0.0 collective-permute-done.5.refs_6_
  236.7 0.0 collective-permute-done.1.refs_3_
  236.7 2.9 %collective-permute-done.2.refs_4_ = bf16[4,128,256]{2,1,0:T(8,128)(2,1)S(1)} collective-permute-done((bf16[4,128,256]{2,1,0:T(8,128)(2,1)S(1)}, bf16[4,128,256]{2,1,0:T(8,128)(2,1)S(1)}, u32[]{:S(2)}, u32[]{:S(2)}) %collective-permute-start.2) | collective-permute-done | bytes 262176 | tf_op jit(solution)/shard_map/ppermute | solution.py:328
  239.6 0.0 collective-permute-done.4.refs_5_
  239.7 0.0 copy-done.3
  239.7 0.0 copy-done.4
  239.7 2.0 score.1
  241.6 0.5 collective-permute-start.6
  242.1 4.0 %collective-permute-start.7 = (f32[4,4,128]{2,1,0:T(4,128)S(1)}, f32[4,4,128]{2,1,0:T(4,128)S(1)}, u32[]{:S(2)}, u32[]{:S(2)}) collective-permute-start(f32[4,4,128]{2,1,0:T(4,128)S(1)} %get-tuple-element.26), channel_id=1, source_target_pairs={{0,2},{1,3},{2,0},{3,1},{4,6},{5,7},{6,4},{7,5},{8,10},{9,11},{10,... | collective-permute-start | bytes 24584 | tf_op jit(solution)/shard_map/ppermute | solution.py:328
  246.1 0.0 collective-permute-start.8
  246.1 0.4 collective-permute-done.6.refs_1_
  246.6 1.3 collective-permute-done.7.refs_2_
  247.8 1.9 collective-permute-done.8.refs_3_
  249.8 0.6 collect.1
Async XLA Ops:
  3.5 107.6 %copy-start = (bf16[16,8,128,128]{3,2,1,0:T(8,128)(2,1)S(1)}, bf16[16,8,128,128]{3,2,1,0:T(8,128)(2,1)}, u32[]{:S(2)}) copy-start(bf16[16,8,128,128]{3,2,1,0:T(8,128)(2,1)} %edge_ref.5) | copy-start | bytes 12582916
  114.8 101.7 %copy-start.1 = (f32[2048,256]{1,0:T(8,128)S(1)}, f32[2048,256]{1,0:T(8,128)}, u32[]{:S(2)}) copy-start(f32[2048,256]{1,0:T(8,128)} %param.7) | copy-start | bytes 6291460
  216.4 15.7 %copy-start.2 = (bf16[4,256,256]{2,1,0:T(8,128)(2,1)S(1)}, bf16[4,256,256]{2,1,0:T(8,128)(2,1)}, u32[]{:S(2)}) copy-start(bf16[4,256,256]{2,1,0:T(8,128)(2,1)} %weight_ref.1) | copy-start | bytes 1572868
  218.5 10.4 %collective-permute-start = (bf16[4,128,256]{2,1,0:T(8,128)(2,1)S(1)}, bf16[4,128,256]{2,1,0:T(8,128)(2,1)S(1)}, u32[]{:S(2)}, u32[]{:S(2)}) collective-permute-start(bf16[4,128,256]{2,1,0:T(8,128)(2,1)S(1)} %get-tuple-element.22.refs_0_), channel_id=1, source_target_pairs={{0,1},{1,2},{2,3},{3,0},{4,5},{5,6},{6,7},{7,4},{8,9},{9,10},{10,1... | collective-permute-start | bytes 786440 | tf_op jit(solution)/shard_map/ppermute | solution.py:328
  218.6 10.3 %collective-permute-start.3 = (bf16[4,128,256]{2,1,0:T(8,128)(2,1)S(1)}, bf16[4,128,256]{2,1,0:T(8,128)(2,1)S(1)}, u32[]{:S(2)}, u32[]{:S(2)}) collective-permute-start(bf16[4,128,256]{2,1,0:T(8,128)(2,1)S(1)} %get-tuple-element.23.refs_1_), channel_id=1, source_target_pairs={{0,3},{1,0},{2,1},{3,2},{4,7},{5,4},{6,5},{7,6},{8,11},{9,8},{10,9... | collective-permute-start | bytes 786440 | tf_op jit(solution)/shard_map/ppermute | solution.py:328
  221.8 14.9 %collective-permute-start.5 = (bf16[4,128,256]{2,1,0:T(8,128)(2,1)S(1)}, bf16[4,128,256]{2,1,0:T(8,128)(2,1)S(1)}, u32[]{:S(2)}, u32[]{:S(2)}) collective-permute-start(bf16[4,128,256]{2,1,0:T(8,128)(2,1)S(1)} %get-tuple-element.22.refs_0_), channel_id=1, source_target_pairs={{0,3},{1,0},{2,1},{3,2},{4,7},{5,4},{6,5},{7,6},{8,11},{9,8},{10,9... | collective-permute-start | bytes 786440 | tf_op jit(solution)/shard_map/ppermute | solution.py:328
  222.1 14.6 %collective-permute-start.1 = (bf16[4,128,256]{2,1,0:T(8,128)(2,1)S(1)}, bf16[4,128,256]{2,1,0:T(8,128)(2,1)S(1)}, u32[]{:S(2)}, u32[]{:S(2)}) collective-permute-start(bf16[4,128,256]{2,1,0:T(8,128)(2,1)S(1)} %get-tuple-element.23.refs_1_), channel_id=1, source_target_pairs={{0,1},{1,2},{2,3},{3,0},{4,5},{5,6},{6,7},{7,4},{8,9},{9,10},{10,1... | collective-permute-start | bytes 786440 | tf_op jit(solution)/shard_map/ppermute | solution.py:328
  228.9 10.8 %collective-permute-start.2 = (bf16[4,128,256]{2,1,0:T(8,128)(2,1)S(1)}, bf16[4,128,256]{2,1,0:T(8,128)(2,1)S(1)}, u32[]{:S(2)}, u32[]{:S(2)}) collective-permute-start(bf16[4,128,256]{2,1,0:T(8,128)(2,1)S(1)} %collective-permute-done.refs_2_), channel_id=1, source_target_pairs={{0,1},{1,2},{2,3},{3,0},{4,5},{5,6},{6,7},{7,4},{8,9},{9,10},{10,1... | collective-permute-start | bytes 786440 | tf_op jit(solution)/shard_map/ppermute | solution.py:328
  228.9 10.8 %collective-permute-start.4 = (bf16[4,128,256]{2,1,0:T(8,128)(2,1)S(1)}, bf16[4,128,256]{2,1,0:T(8,128)(2,1)S(1)}, u32[]{:S(2)}, u32[]{:S(2)}) collective-permute-start(bf16[4,128,256]{2,1,0:T(8,128)(2,1)S(1)} %collective-permute-done.3.refs_7_), channel_id=1, source_target_pairs={{0,3},{1,0},{2,1},{3,2},{4,7},{5,4},{6,5},{7,6},{8,11},{9,8},{10,9... | collective-permute-start | bytes 786440 | tf_op jit(solution)/shard_map/ppermute | solution.py:328
  232.2 7.5 %copy-start.3 = (s32[32,4]{0,1:T(4,128)S(1)}, s32[32,4]{0,1:T(4,128)}, u32[]{:S(2)}) copy-start(s32[32,4]{0,1:T(4,128)} %param.12) | copy-start | bytes 1540
  232.2 7.5 %copy-start.4 = (s32[32,1]{0,1:T(1,128)S(1)}, s32[32,1]{0,1:T(1,128)}, u32[]{:S(2)}) copy-start(s32[32,1]{0,1:T(1,128)} %param.11) | copy-start | bytes 388
  241.6 4.9 %collective-permute-start.6 = (f32[4,4,128]{2,1,0:T(4,128)S(1)}, f32[4,4,128]{2,1,0:T(4,128)S(1)}, u32[]{:S(2)}, u32[]{:S(2)}) collective-permute-start(f32[4,4,128]{2,1,0:T(4,128)S(1)} %get-tuple-element.25), channel_id=1, source_target_pairs={{0,1},{1,2},{2,3},{3,0},{4,5},{5,6},{6,7},{7,4},{8,9},{9,10},{10,1... | collective-permute-start | bytes 24584 | tf_op jit(solution)/shard_map/ppermute | solution.py:328
  242.1 5.7 %collective-permute-start.7 = (f32[4,4,128]{2,1,0:T(4,128)S(1)}, f32[4,4,128]{2,1,0:T(4,128)S(1)}, u32[]{:S(2)}, u32[]{:S(2)}) collective-permute-start(f32[4,4,128]{2,1,0:T(4,128)S(1)} %get-tuple-element.26), channel_id=1, source_target_pairs={{0,2},{1,3},{2,0},{3,1},{4,6},{5,7},{6,4},{7,5},{8,10},{9,11},{10,... | collective-permute-start | bytes 24584 | tf_op jit(solution)/shard_map/ppermute | solution.py:328
  246.1 3.7 %collective-permute-start.8 = (f32[4,4,128]{2,1,0:T(4,128)S(1)}, f32[4,4,128]{2,1,0:T(4,128)S(1)}, u32[]{:S(2)}, u32[]{:S(2)}) collective-permute-start(f32[4,4,128]{2,1,0:T(4,128)S(1)} %get-tuple-element.27), channel_id=1, source_target_pairs={{0,3},{1,0},{2,1},{3,2},{4,7},{5,4},{6,5},{7,6},{8,11},{9,8},{10,9... | collective-permute-start | bytes 24584 | tf_op jit(solution)/shard_map/ppermute | solution.py:328
